TPU v7x, 32 devices: a whole 2x2x4 slice. The times are simulated.
32 devices in a mesh: dp: 4 (over x, core), row: 2 (over y), col: 4 (over z).
Axes of the slice: x: 2, y: 2, z: 4, core: 2. Of those that a mesh axis runs over, the one named last changes fastest.
Arguments:
- tokens: bfloat16 [8192, 1024], P(('dp', 'col'), 'row'), may hold values from -6 to 6
- segments: int32 [8192], P('dp'), may hold values from 0 to 17, as said below
- triple_weight: bfloat16 [1024, 3, 1024], P('row', None, 'col'), may hold values from -0.25 to 0.25
- pair_bias: bfloat16 [2, 1024], P(None, 'col'), may hold values from -3 to 3
- merge_weight: bfloat16 [1024, 1024], P('col', 'row'), may hold values from -1.5 to 1.5
- merge_bias: bfloat16 [1024], P('row'), may hold values from -2 to 2
- first_gain: bfloat16 [1024], P('row'), may hold values from 0.5 to 1.5
- first_shift: bfloat16 [1024], P('row'), may hold values from -3 to 3
- expand_weight: bfloat16 [1024, 4096], P('row', 'col'), may hold values from -0.1875 to 0.1875
- expand_bias: bfloat16 [4096], P('col'), may hold values from -3 to 3
- shrink_weight: bfloat16 [4096, 1024], P('col', 'row'), may hold values from -0.09375 to 0.09375
- shrink_bias: bfloat16 [1024], P('row'), may hold values from -2 to 2
- second_gain: bfloat16 [1024], P('row'), may hold values from 0.5 to 1.5
- second_shift: bfloat16 [1024], P('row'), may hold values from -3 to 3
- cotangent: bfloat16 [8192, 1024], P(('dp', 'col'), 'row'), may hold values from -6 to 6
Outputs:
- layer_out: bfloat16 [8192, 1024], P(('dp', 'col'), 'row')
- grad_tokens: float32 [8192, 1024], P(('dp', 'col'), 'row')
- grad_triple: float32 [1024, 3, 1024], P('row', None, 'col')
- grad_pair: float32 [2, 1024], P(None, 'col')
- grad_merge: float32 [1024, 1024], P('col', 'row')
- grad_merge_bias: float32 [1024], P('row')
- grad_first_gain: float32 [1024], P('row')
- grad_first_shift: float32 [1024], P('row')
- grad_expand: float32 [1024, 4096], P('row', 'col')
- grad_expand_bias: float32 [4096], P('col')
- grad_shrink: float32 [4096, 1024], P('col', 'row')
- grad_shrink_bias: float32 [1024], P('row')
- grad_second_gain: float32 [1024], P('row')
- grad_second_shift: float32 [1024], P('row')
Inputs may be any that keep to these rules, and one draw needn't show every extreme that they name: `segments`: within each sequence of 1024 consecutive tokens the numbers are 1, 2, 3, ... over whole documents of 60 to 800 tokens, followed by 0 on a trailing pad of fewer than 800 tokens; some document holds exactly 800 tokens.
All inputs are finite; a program needn't handle non-finite values.
Results may differ from a plain program's by a relative error of at most 0.017.
The roundings to bfloat16 on the way count: a program that leaves them out, or rounds other values in their place, can miss the bound.
Values may be sent and summed in bfloat16 or wider, within the bound.
No kernel may reach another device: no remote copies, remote signals or barrier semaphores. Data moves between devices by JAX's collectives and lax.ppermute only.
A program may use at most 192 MiB of HBM per device.

v0:
```python
import functools

import jax
import jax.numpy as jnp
from jax import lax
from jax.experimental import pallas as pl
from jax.experimental.pallas import tpu as pltpu
from jax.sharding import Mesh, PartitionSpec as P

D = 1024
HEAD = 64
LEN = 1024
epsilon = 1e-05
masked_score = -1e30
bf16 = jnp.bfloat16
f32 = jnp.float32


def size(axis):
    return lax.axis_size(axis)


def place(axis):
    return lax.axis_index(axis)


def pair(values, axis):
    return lax.ppermute(values, axis, [(0, 1), (1, 0)])


def after(values, *others):
    return lax.optimization_barrier((values,) + others)[0]


def together(*arrays):
    return lax.optimization_barrier(arrays)


def shift(values, step):
    count = size("col")
    return lax.ppermute(values, "col", [(i, (i + step) % count) for i in range(count)])


def across(values, bits):
    return lax.ppermute(values, "col", [(i, i ^ bits) for i in range(size("col"))])


def by_place(bit, own, other, axis):
    return jnp.where(
        bit == 0,
        jnp.concatenate((own, other), axis),
        jnp.concatenate((other, own), axis),
    )


def nt(left, right, kind=f32):
    return lax.dot_general(
        left, right, (((1,), (1,)), ((), ())), preferred_element_type=f32
    ).astype(kind)


def nn(left, right, kind=f32):
    return lax.dot_general(
        left, right, (((1,), (0,)), ((), ())), preferred_element_type=f32
    ).astype(kind)


def tn(left, right, kind=f32):
    return lax.dot_general(
        left, right, (((0,), (0,)), ((), ())), preferred_element_type=f32
    ).astype(kind)


def swap_sequences(values):
    count = size("col")
    perm = []
    for core in range(2):
        for col in range(count):
            half, other = col % 2, col - col % 2
            target = (half, other + core)
            perm.append((core * count + col, target[0] * count + target[1]))
    return lax.ppermute(values, ("core", "col"), perm)


def own_first(values):
    if size("row") != 2:
        return values
    half = values.shape[0] // 2
    return jnp.where(place("row") == 0, values, jnp.roll(values, half, axis=0))


def own_part(values):
    share = values.shape[0] // size("row")
    if size("row") == 2:
        return values[:share]
    return lax.dynamic_slice_in_dim(values, place("row") * share, share)


def gather_features(values):
    if size("row") == 2:
        full = by_place(place("row"), values, pair(values, "row"), 1)
        return own_first(full)
    return lax.all_gather(values, "row", axis=1, tiled=True)


def gather_tokens(values):
    if size("row") == 2:
        return jnp.concatenate((values, pair(values, "row")), 0)
    return lax.all_gather(values, "row", axis=0, tiled=True)


def sum_tokens(partial):
    if size("row") == 2:
        share = partial.shape[0] // 2
        return partial[:share] + pair(partial[share:].astype(bf16), "row").astype(f32)
    return lax.psum_scatter(partial, "row", scatter_dimension=0, tiled=True)


def to_own_tokens(values):
    if size("row") == 2:
        bit = place("row")
        ordered = own_first(values)
        share = values.shape[0] // 2
        return by_place(bit, ordered[:share], pair(ordered[share:], "row"), 1)
    return lax.all_to_all(values, "row", 0, 1, tiled=True)


def to_own_features(values):
    if size("row") == 2:
        bit = place("row")
        half = values.shape[1] // 2
        low, high = values[:, :half], values[:, half:]
        own = jnp.where(bit == 0, low, high)
        other = pair(jnp.where(bit == 0, high, low), "row")
        return by_place(bit, own, other, 0)
    return lax.all_to_all(values, "row", 1, 0, tiled=True)


def sum_features(partial, addend):
    if size("row") == 2:
        half = partial.shape[1] // 2
        low, high = partial[:, :half], partial[:, half:]
        bit = place("row")
        got = pair(jnp.where(bit == 0, high, low).astype(bf16), "row").astype(f32)
        got = jnp.roll(got, partial.shape[0] // 2, axis=0)
        return own_first(jnp.where(bit == 0, low, high) + got) + addend
    return lax.psum_scatter(partial, "row", scatter_dimension=1, tiled=True) + addend


class Held:
    def __init__(self, **arrays):
        vars(self).update(arrays)

    update = __init__


def step_of(held):
    return Held(**lax.optimization_barrier(vars(held)))


def halves(values):
    middle = values.shape[0] // 2
    return values[:middle], values[middle:]


def three_groups(triple, merge, expand, shrink):
    depth = triple.shape[0]
    heads = triple.transpose(1, 2, 0).reshape(3, 2, 2, 1, HEAD, depth)
    out = merge.reshape(1, 2, 2, 1, HEAD, depth)
    keys_values = jnp.concatenate((heads[1], heads[2]), 3 - 1)
    queries_merge = jnp.concatenate((heads[0], out[0]), 3 - 1)
    attend = jnp.stack((keys_values, queries_merge), 2).reshape(2, 2, 2, 2 * HEAD, depth)
    widen = expand.T.reshape(2, 2, 2, -1, depth)
    narrow = shrink.reshape(2, 2, 2, -1, depth)
    return attend, widen, narrow


def my_quarter(group):
    some = lax.dynamic_index_in_dim(group, place("outer"), 1, keepdims=False)
    return lax.dynamic_index_in_dim(some, place("core"), 1, keepdims=False)


def exchange_rows(quarter):
    bit = place("row")
    mine = jnp.where(bit == 0, quarter[0], quarter[1])
    other = pair(jnp.where(bit == 0, quarter[1], quarter[0]), "row")
    return by_place(bit, mine, other, 1)


STEPS = (1, 3, 2)
BACK = (2, 1, 3)


def own_core_half(parts, pairs):
    count = size("col")
    return jnp.stack(
        [jnp.stack([group[step] for step in range(count)]) for group in (parts, pairs)]
    )


def gather_attend(quarter):
    parts = {0: quarter}
    for step in STEPS:
        parts[step] = shift(quarter, step)
    pairs = {step: pair(parts[step], "outer") for step in (0,) + STEPS}
    return own_core_half(parts, pairs), parts[2], pairs[2]


def collect_row(last):
    bit = place("row")
    half = last.shape[1] // 2
    low, high = last[:, :half].astype(bf16), last[:, half:].astype(bf16)
    mine = jnp.where(bit == 0, low, high)
    got = pair(jnp.where(bit == 0, high, low), "row")
    return jnp.stack((jnp.where(bit == 0, mine, got), jnp.where(bit == 0, got, mine)))


def ungroup(attend):
    depth = attend.shape[-1]
    heads = attend.reshape(4, 2, 2, HEAD, depth)
    keys, values = heads[:, 0, 0], heads[:, 0, 1]
    queries, merge = heads[:, 1, 0], heads[:, 1, 1]
    triple = jnp.stack((queries, keys, values)).reshape(3, 4 * HEAD, depth).transpose(2, 0, 1)
    return triple, merge.reshape(4 * HEAD, depth)


def flip(values, axis, bit):
    return jnp.where(bit == 0, values, jnp.flip(values, axis))


def dot(left, right, left_dim, right_dim):
    return lax.dot_general(
        left, right, (((left_dim,), (right_dim,)), ((), ())), preferred_element_type=f32
    )


def params():
    return pltpu.CompilerParams(vmem_limit_bytes=36 << 20)


def anywhere(arrays):
    return [pl.BlockSpec(memory_space=pl.ANY) for _ in arrays]


def pick(near_ref, far_ref, begin):
    part = slice(begin, begin + HEAD)
    return jnp.concatenate((near_ref[:, part], far_ref[:, part]), 0)


def attend_forward_kernel(q_ref, near_ref, far_ref, qs_ref, ks_ref, out_ref, lse_ref):
    same = ks_ref[...] == qs_ref[...]
    for head in range(2):
        part = slice(head * HEAD, (head + 1) * HEAD)
        keys = pick(near_ref, far_ref, 2 * head * HEAD)
        values = pick(near_ref, far_ref, (2 * head + 1) * HEAD)
        queries = q_ref[:, part] * jnp.asarray(HEAD**-0.5, bf16)
        scores = jnp.where(same, dot(keys, queries, 1, 1), masked_score)
        top = jnp.max(scores, axis=0, keepdims=True)
        weights = jnp.exp(scores - top)
        total = jnp.sum(weights, axis=0, keepdims=True)
        low = (weights * (1.0 / total)).astype(bf16)
        out_ref[part] = dot(values, low, 0, 0).astype(bf16)
        lse_ref[0, head : head + 1] = top + jnp.log(total)


def attend_forward(queries, near, far, query_segment, key_segment):
    tokens, width = queries.shape
    steps = width // (2 * HEAD)
    block = pl.BlockSpec((tokens, 4 * HEAD), lambda i: (0, i))
    return pl.pallas_call(
        attend_forward_kernel,
        grid=(steps,),
        in_specs=[
            pl.BlockSpec((tokens, 2 * HEAD), lambda i: (0, i)),
            block,
            block,
            pl.BlockSpec((1, tokens), lambda i: (0, 0)),
            pl.BlockSpec((2 * tokens, 1), lambda i: (0, 0)),
        ],
        out_specs=[
            pl.BlockSpec((2 * HEAD, tokens), lambda i: (i, 0)),
            pl.BlockSpec((1, 2, tokens), lambda i: (i, 0, 0)),
        ],
        out_shape=[
            jax.ShapeDtypeStruct((width, tokens), bf16),
            jax.ShapeDtypeStruct((steps, 2, tokens), f32),
        ],
        compiler_params=params(),
        cost_estimate=pl.CostEstimate(
            flops=32 * tokens * tokens * width,
            bytes_accessed=4 << 20,
            transcendentals=2 * tokens * tokens * width // HEAD,
        ),
    )(queries, near, far, query_segment, key_segment)


def attend_backward_kernel(
    q_ref, kv_ref, far_kv_ref, g_ref, qs_ref, ks_ref, lse_ref, dq_ref, near_ref, far_ref
):
    same = ks_ref[...] == qs_ref[...]
    scale = HEAD**-0.5
    near = near_ref.shape[0]
    for head in range(2):
        part = slice(head * HEAD, (head + 1) * HEAD)
        key_part = slice(2 * head * HEAD, (2 * head + 1) * HEAD)
        value_part = slice((2 * head + 1) * HEAD, (2 * head + 2) * HEAD)
        keys = pick(kv_ref, far_kv_ref, key_part.start)
        values = pick(kv_ref, far_kv_ref, value_part.start)
        queries = q_ref[:, part] * jnp.asarray(scale, bf16)
        grad = g_ref[:, part]
        scores = jnp.where(same, dot(keys, queries, 1, 1), masked_score)
        weights = jnp.exp(scores - lse_ref[0, head : head + 1])
        grad_weights = dot(values, grad, 1, 1)
        inner = jnp.sum(weights * grad_weights, axis=0, keepdims=True)
        grad_scores = (weights * (grad_weights - inner)).astype(bf16)
        dq_ref[part] = (dot(keys, grad_scores, 0, 0) * scale).astype(bf16)
        grad_keys = dot(grad_scores, queries, 1, 0)
        grad_values = dot(weights.astype(bf16), grad, 1, 0)
        near_ref[:, key_part], far_ref[:, key_part] = grad_keys[:near], grad_keys[near:]
        near_ref[:, value_part], far_ref[:, value_part] = grad_values[:near], grad_values[near:]


def attend_backward(queries, near, far, grad, query_segment, key_segment, lse, begin, steps):
    tokens = queries.shape[0]
    block = pl.BlockSpec((tokens, 4 * HEAD), lambda i: (0, begin + i))
    query_block = pl.BlockSpec((tokens, 2 * HEAD), lambda i: (0, begin + i))
    key_block = pl.BlockSpec((tokens, 4 * HEAD), lambda i: (0, i))
    return pl.pallas_call(
        attend_backward_kernel,
        grid=(steps,),
        in_specs=[
            query_block,
            block,
            block,
            query_block,
            pl.BlockSpec((1, tokens), lambda i: (0, 0)),
            pl.BlockSpec((2 * tokens, 1), lambda i: (0, 0)),
            pl.BlockSpec((1, 2, tokens), lambda i: (begin + i, 0, 0)),
        ],
        out_specs=[pl.BlockSpec((2 * HEAD, tokens), lambda i: (i, 0)), key_block, key_block],
        out_shape=[
            jax.ShapeDtypeStruct((2 * HEAD * steps, tokens), bf16),
            jax.ShapeDtypeStruct((tokens, 4 * HEAD * steps), f32),
            jax.ShapeDtypeStruct((tokens, 4 * HEAD * steps), f32),
        ],
        compiler_params=params(),
        cost_estimate=pl.CostEstimate(
            flops=160 * tokens * tokens * steps * HEAD,
            bytes_accessed=8 << 20,
            transcendentals=4 * tokens * tokens * steps,
        ),
    )(queries, near, far, grad, query_segment, key_segment, lse)


def attend_weights_kernel(
    which_ref, dkv_ref, dq_ref, out_in_ref, x_ref, g_ref, *rest, added, cols
):
    add_ref = rest[0] if added else None
    out_refs = rest[-cols:]

    def put(rows, value):
        value = value.reshape(cols, -1, D)
        for step, out_ref in enumerate(out_refs):
            term = value[step]
            if added:
                term = term + add_ref[0, step, rows].astype(f32)
            out_ref[rows] = term.astype(out_ref.dtype)

    @pl.when(which_ref[0] == 0)
    def _():
        put(slice(0, 2 * HEAD), dot(dkv_ref[...], x_ref[...], 0, 0))

    @pl.when(which_ref[0] == 1)
    def _():
        put(slice(0, HEAD), dot(dq_ref[...], x_ref[...], 1, 0))
        put(slice(HEAD, 2 * HEAD), dot(out_in_ref[...], g_ref[...], 1, 0))


def attend_weights(which, dkv, dq, out_in, x, g, begin, cols, kind, add=None, earlier=()):
    tokens = x.shape[0]
    full = pl.BlockSpec((tokens, D), lambda i, w: (0, 0))
    rows = pl.BlockSpec((cols * HEAD, tokens), lambda i, w: (begin, 0))
    specs = [pl.BlockSpec((tokens, cols * 2 * HEAD), lambda i, w: (0, begin)), rows, rows, full, full]
    given = [dkv, dq, out_in, x, g]
    if add is not None:
        specs.append(pl.BlockSpec((1, cols, 2 * HEAD, D), lambda i, w: (begin, 0, 0, 0)))
        given.append(add)
    return pl.pallas_call(
        functools.partial(attend_weights_kernel, added=add is not None, cols=cols),
        grid_spec=pltpu.PrefetchScalarGridSpec(
            num_scalar_prefetch=1,
            grid=(1,),
            in_specs=specs + anywhere(earlier),
            out_specs=[pl.BlockSpec((2 * HEAD, D), lambda i, w: (0, 0))] * cols,
        ),
        out_shape=[jax.ShapeDtypeStruct((2 * HEAD, D), kind)] * cols,
        compiler_params=params(),
        cost_estimate=pl.CostEstimate(
            flops=4 * tokens * D * cols * HEAD, bytes_accessed=6 << 20, transcendentals=0
        ),
    )(which, *given, *earlier)


def attend_far_kernel(which_ref, dkv_ref, dq_ref, out_in_ref, x_ref, g_ref, *rest):
    out_ref = rest[-1]
    cols = out_ref.shape[1]

    @pl.when(which_ref[0] == 0)
    def _():
        value = dot(dkv_ref[...], x_ref[...], 0, 0)
        out_ref[0] = value.reshape(cols, 2 * HEAD, D).astype(out_ref.dtype)

    @pl.when(which_ref[0] == 1)
    def _():
        for part, value in enumerate(
            (dot(dq_ref[...], x_ref[...], 1, 0), dot(out_in_ref[...], g_ref[...], 1, 0))
        ):
            rows = slice(part * HEAD, (part + 1) * HEAD)
            out_ref[0, :, rows] = value.reshape(cols, HEAD, D).astype(out_ref.dtype)


def attend_far_weights(which, dkv, dq, out_in, x, g, cols, *earlier):
    tokens = x.shape[0]
    full = pl.BlockSpec((tokens, D), lambda i, w: (0, 0))
    rows = pl.BlockSpec((cols * HEAD, tokens), lambda i, w: (i, 0))
    return pl.pallas_call(
        attend_far_kernel,
        grid_spec=pltpu.PrefetchScalarGridSpec(
            num_scalar_prefetch=1,
            grid=(2,),
            in_specs=[
                pl.BlockSpec((tokens, cols * 2 * HEAD), lambda i, w: (0, i)), rows, rows, full, full
            ]
            + anywhere(earlier),
            out_specs=pl.BlockSpec((1, cols, 2 * HEAD, D), lambda i, w: (i, 0, 0, 0)),
        ),
        out_shape=jax.ShapeDtypeStruct((2, cols, 2 * HEAD, D), bf16),
        compiler_params=params(),
        cost_estimate=pl.CostEstimate(
            flops=8 * tokens * D * cols * HEAD, bytes_accessed=6 << 20, transcendentals=0
        ),
    )(which, dkv, dq, out_in, x, g, *earlier)


SPARE = 8


def units_of(weights):
    units = (weights.shape[2] - SPARE) // 2
    expand = weights[:, :, :units].reshape(-1, D)
    shrink = weights[:, :, units : 2 * units].reshape(-1, D)
    return expand, shrink


def finish(total, keep_ref, send_ref):
    @pl.when(pl.program_id(0) == pl.num_programs(0) - 1)
    def _():
        half = total.shape[0] // 2
        keep_ref[...] = total[:half]
        send_ref[...] = total[half:].astype(bf16)


def add_to(total, term):
    @pl.when(pl.program_id(0) == 0)
    def _():
        total[...] = term

    @pl.when(pl.program_id(0) > 0)
    def _():
        total[...] += term


def hidden_forward_kernel(
    x_ref, bias_ref, weights_ref, hidden_ref, slope_ref, keep_ref, send_ref, total
):
    expand, shrink = units_of(weights_ref[0, 0:1])
    u = dot(x_ref[...], expand, 1, 1) + bias_ref[0]
    normal = 0.5 * (1.0 + lax.erf(u * (0.5**0.5)))
    slope_ref[...] = normal + u * (jnp.exp(-0.5 * u * u) * ((0.5 / jnp.pi) ** 0.5))
    hidden = (u * normal).astype(bf16)
    hidden_ref[...] = hidden
    add_to(total, dot(hidden, shrink, 1, 0))
    finish(total, keep_ref, send_ref)


def hidden_specs(tokens, weights):
    outer, core, cols, rows, _ = weights.shape
    units = (rows - SPARE) // 2
    steps, width = outer * core, cols * units
    block = pl.BlockSpec((1, 1, cols, rows, D), lambda i: (i // core, i % core, 0, 0, 0))
    wide = pl.BlockSpec((tokens, width), lambda i: (0, i))
    half = pl.BlockSpec((tokens // 2, D), lambda i: (0, 0))
    half_shapes = [
        jax.ShapeDtypeStruct((tokens // 2, D), f32),
        jax.ShapeDtypeStruct((tokens // 2, D), bf16),
    ]
    full = pl.BlockSpec((tokens, D), lambda i: (0, 0))
    row = pl.BlockSpec((1, 1, width), lambda i: (i, 0, 0))
    cost = pl.CostEstimate(
        flops=4 * tokens * D * steps * width, bytes_accessed=20 << 20, transcendentals=0
    )
    return steps, width, block, wide, half, half_shapes, full, row, cost


def hidden_forward(x, weights, bias):
    tokens = x.shape[0]
    steps, width, block, wide, half, half_shapes, full, row, cost = hidden_specs(tokens, weights)
    shape = (tokens, steps * width)
    return pl.pallas_call(
        hidden_forward_kernel,
        grid=(steps,),
        in_specs=[full, row, block],
        out_specs=[wide, wide, half, half],
        out_shape=[jax.ShapeDtypeStruct(shape, bf16), jax.ShapeDtypeStruct(shape, f32)]
        + half_shapes,
        scratch_shapes=[pltpu.VMEM((tokens, D), f32)],
        compiler_params=params(),
        cost_estimate=cost,
    )(x, bias, weights)


def hidden_backward_kernel(
    g_ref, slope_ref, weights_ref, grad_ref, sum_ref, keep_ref, send_ref, total
):
    expand, shrink = units_of(weights_ref[0, 0:1])
    grad = (dot(g_ref[...], shrink, 1, 1) * slope_ref[...]).astype(bf16)
    grad_ref[...] = grad
    sum_ref[0] = jnp.sum(grad.astype(f32), axis=0, keepdims=True)
    add_to(total, dot(grad, expand, 1, 0))
    finish(total, keep_ref, send_ref)


def hidden_backward(g, weights, slope):
    tokens = g.shape[0]
    steps, width, block, wide, half, half_shapes, full, row, cost = hidden_specs(tokens, weights)
    return pl.pallas_call(
        hidden_backward_kernel,
        grid=(steps,),
        in_specs=[full, wide, block],
        out_specs=[wide, row, half, half],
        out_shape=[
            jax.ShapeDtypeStruct((tokens, steps * width), bf16),
            jax.ShapeDtypeStruct((steps, 1, width), f32),
        ]
        + half_shapes,
        scratch_shapes=[pltpu.VMEM((tokens, D), f32)],
        compiler_params=params(),
        cost_estimate=cost,
    )(g, slope, weights)


def hidden_weights_kernel(grad_ref, hidden_ref, x_ref, g_ref, sum_ref, out_ref):
    cols, rows, _ = out_ref.shape[2:]
    units = (rows - SPARE) // 2
    for part, (left, right) in enumerate(((grad_ref, x_ref), (hidden_ref, g_ref))):
        value = dot(left[...], right[...], 0, 0).reshape(cols, units, D)
        out_ref[0, 0, :, part * units : (part + 1) * units] = value.astype(bf16)
    first = lax.broadcasted_iota(jnp.int32, (cols, SPARE, units), 1) == 0
    sums = jnp.where(first, sum_ref[0][:, None, :], 0.0).astype(bf16)
    out_ref[0, 0, :, 2 * units :] = jnp.zeros((cols, SPARE, D), bf16)
    for begin in (0, D // 2):
        out_ref[0, 0, :, 2 * units :, begin : begin + units] = sums


def hidden_weights(grad, hidden, x, g, sums, shape):
    tokens = x.shape[0]
    outer, core, cols, rows, _ = shape
    width = grad.shape[1] // (outer * core)
    wide = pl.BlockSpec((tokens, width), lambda i: (0, i))
    full = pl.BlockSpec((tokens, D), lambda i: (0, 0))
    return pl.pallas_call(
        hidden_weights_kernel,
        grid=(outer * core,),
        in_specs=[
            wide, wide, full, full, pl.BlockSpec((1, cols, width // cols), lambda i: (i, 0, 0))
        ],
        out_specs=pl.BlockSpec(
            (1, 1, cols, rows, D), lambda i: (i // core, i % core, 0, 0, 0)
        ),
        out_shape=jax.ShapeDtypeStruct(shape, bf16),
        compiler_params=params(),
        cost_estimate=pl.CostEstimate(
            flops=4 * tokens * D * grad.shape[1], bytes_accessed=16 << 20, transcendentals=0
        ),
    )(grad, hidden, x, g, sums)


def hidden_gradients_kernel(core_ref, own_ref, got_ref, expand_ref, shrink_ref, bias_ref):
    units = shrink_ref.shape[0]

    def put(ref):
        expand_ref[...] = ref[0, 0, :units].astype(f32).T
        shrink_ref[...] = ref[0, 0, units : 2 * units].astype(f32)
        bias_ref[0] = ref[0, 0, 2 * units :, :units].astype(f32)

    mine = pl.program_id(0) % 2 == core_ref[0]
    pl.when(mine)(lambda: put(own_ref))
    pl.when(jnp.logical_not(mine))(lambda: put(got_ref))


def hidden_gradients(core, own, got):
    rows, depth = own.shape[2:]
    units = (rows - SPARE) // 2
    piece = pl.BlockSpec((1, 1, rows, depth), lambda i, w: (i // 4, i // 2 % 2, 0, 0))
    expand, shrink, bias = pl.pallas_call(
        hidden_gradients_kernel,
        grid_spec=pltpu.PrefetchScalarGridSpec(
            num_scalar_prefetch=1,
            grid=(8,),
            in_specs=[piece, piece],
            out_specs=[
                pl.BlockSpec((depth, units), lambda i, w: (0, i)),
                pl.BlockSpec((units, depth), lambda i, w: (i, 0)),
                pl.BlockSpec((1, SPARE, units), lambda i, w: (i, 0, 0)),
            ],
        ),
        out_shape=[
            jax.ShapeDtypeStruct((depth, 8 * units), f32),
            jax.ShapeDtypeStruct((8 * units, depth), f32),
            jax.ShapeDtypeStruct((8, SPARE, units), f32),
        ],
        compiler_params=params(),
        cost_estimate=pl.CostEstimate(flops=1 << 20, bytes_accessed=6 << 20, transcendentals=0),
    )(core, own, got)
    return expand, shrink, bias[:, 0].reshape(-1)


def layer(
    tokens, segments, triple_weight, pair_bias, merge_weight, merge_bias, first_gain, first_shift,
    expand_weight, expand_bias, shrink_weight, shrink_bias, second_gain, second_shift, cotangent,
):
    cols = size("col")
    count = tokens.shape[0]
    own = count // 2
    heads = D // HEAD // 2
    row, col, core, outer = place("row"), place("col"), place("core"), place("outer")
    row_size, pair_size, hidden_size = merge_bias.shape[0], pair_bias.shape[1], expand_bias.shape[0]

    groups = three_groups(triple_weight, merge_weight, expand_weight, shrink_weight)
    attend_group = my_quarter(groups[0])
    row_vectors = jnp.stack(
        (merge_bias, first_gain, first_shift, shrink_bias, second_gain, second_shift)
    )
    column = jnp.concatenate(
        [
            lax.dynamic_slice_in_dim(vector, row * (vector.shape[0] // 2), vector.shape[0] // 2)
            for vector in (pair_bias[0], pair_bias[1], expand_bias)
        ]
    )
    moved = swap_sequences(tokens)
    quarter = exchange_rows(attend_group)
    pair_column, hidden_column = column[:pair_size], column[pair_size:].reshape(4, -1)
    pair_column = pair_column.reshape(2, 2, HEAD)
    pair_column = lax.dynamic_index_in_dim(pair_column, outer, 1, keepdims=False)
    pair_column = lax.dynamic_index_in_dim(pair_column, 1 - core, 0)
    hidden_column = lax.dynamic_index_in_dim(hidden_column, 2 * outer + core, 0)
    other_group = exchange_rows(
        jnp.concatenate([my_quarter(group) for group in groups[1:]], 1)
    )
    v = step_of(
        Held(
            quarter=quarter, moved=moved, other=segments.astype(f32), group=other_group, rows=row_vectors, pairs=pair_column,
            hidden=hidden_column, cot=cotangent,
        )
    )

    def beside(rows, value):
        spare = jnp.pad(value, ((0, SPARE - 1), (0, D - value.shape[1])))
        return jnp.concatenate((rows, spare), 0)

    quarter, moved = beside(v.quarter, v.pairs), v.moved
    parts = {0: quarter, 1: shift(quarter, 1), 3: shift(quarter, 3)}
    pairs = {0: pair(quarter, "outer")}
    got_tokens = pair(moved, "row")
    v.update(quarter=quarter, parts=parts, pairs=pairs, moved=moved, got=got_tokens)
    v = step_of(v)
    parts, pairs, quarter = v.parts, v.pairs, v.quarter
    parts[2] = shift(quarter, 2)
    pairs[1], pairs[3] = pair(parts[1], "outer"), pair(parts[3], "outer")
    mine = beside(v.group, v.hidden)
    hidden_all = lax.all_gather(mine, ("outer", "core", "col"), axis=0)
    hidden_all = hidden_all.reshape(2, 2, cols, -1, D)
    v.vectors = by_place(row, v.rows, pair(v.rows, "row"), 1)
    v.other = pair(v.other, "core")
    v = step_of(v)
    parts, pairs = v.parts, v.pairs
    pairs[2] = pair(parts[2], "outer")
    v.inputs = own_first(by_place(row, v.moved, v.got, 1))
    v = step_of(v)
    parts, pairs = v.parts, v.pairs
    rows = 2 * HEAD

    def without(group):
        return {step: group[step][:rows] for step in range(cols)}

    attend_own = own_core_half(without(parts), without(pairs))
    v.attend_own, v.attend_other = attend_own, pair(attend_own, "core")
    bias_own = jnp.stack(
        [group[step][rows, :HEAD] for group in (parts, pairs) for step in range(cols)]
    ).astype(f32)
    v.bias_own, v.bias_other = bias_own, pair(bias_own, "core")
    other = v.other.astype(jnp.int32)
    sequence = lax.dynamic_slice_in_dim(
        jnp.where(col % 2 == core, segments, other), (col // 2) * LEN, LEN
    ).reshape(2, count)
    query_segment = own_first(lax.dynamic_index_in_dim(sequence, core, 0, keepdims=False))
    far_segment = own_first(lax.dynamic_index_in_dim(sequence, 1 - core, 0, keepdims=False))
    key_segment = jnp.concatenate((query_segment, far_segment))
    segment_row, segment_column = query_segment[None], key_segment[:, None]
    vectors = v.vectors.astype(f32)
    v = step_of(
        Held(
            own=v.attend_own, other=v.attend_other, cot=v.cot, inputs=v.inputs,
            vectors=vectors, biases=(v.bias_own, v.bias_other),
        )
    )
    attend_own, attend_other, inputs, vectors = v.own, v.other, v.inputs, v.vectors
    first = jnp.where(core == 0, attend_own, attend_other)
    second = jnp.where(core == 0, attend_other, attend_own)
    bias_values = jnp.where(core == 0, v.biases[0], v.biases[1])
    bias_keys_values = jnp.stack((jnp.zeros_like(bias_values), bias_values), 1).reshape(-1)
    bias_queries = jnp.where(core == 0, v.biases[1], v.biases[0]).reshape(-1)
    weight_keys_values = first.reshape(-1, D)
    second = second.reshape(heads, 2, HEAD, D)
    weight_queries, weight_merge = second[:, 0].reshape(-1, D), second[:, 1].reshape(-1, D)

    cut = heads * HEAD // 2
    steps = heads // 4
    keys_values = (nt(inputs, weight_keys_values) + bias_keys_values).astype(bf16)
    v.far = pair(keys_values, "core")
    v.queries = (nt(inputs, weight_queries) + bias_queries).astype(bf16)
    v.keys_values = keys_values
    v.weights = (weight_keys_values, weight_queries, weight_merge)
    v = step_of(v)
    queries = v.queries
    keys_values, far_keys_values = v.keys_values, v.far
    v.attended, v.lse = attend_forward(
        queries, keys_values, far_keys_values, segment_row, segment_column
    )
    v = step_of(v)
    attended, lse = v.attended, v.lse
    queries, keys_values, far_keys_values = v.queries, v.keys_values, v.far
    weight_keys_values, weight_queries, weight_merge = v.weights
    branch = sum_tokens(tn(attended, weight_merge))
    residual = inputs[:own].astype(f32) + (branch + vectors[0])
    scaled_one, inverse_one, normed_one = norm_forward(residual, vectors[1], vectors[2])
    normed_low = gather_tokens(normed_one.astype(bf16))
    cotangent = swap_sequences(v.cot)
    normed_low, normed_one, hidden_all, cotangent = lax.optimization_barrier(
        (normed_low, normed_one, hidden_all, cotangent)
    )
    units = hidden_size // 8
    bias_hidden = hidden_all[:, :, :, 2 * units, :units].reshape(4, 1, -1).astype(f32)
    hidden, slope, keep, send = hidden_forward(normed_low, hidden_all, bias_hidden)
    upstream = to_own_tokens(cotangent)
    keep, send, upstream = lax.optimization_barrier((keep, send, upstream))
    shrunk = keep + pair(send, "row").astype(f32)
    scaled_two, inverse_two, final = norm_forward(
        normed_one + (shrunk + vectors[3]), vectors[4], vectors[5]
    )
    live = (query_segment[:own] != 0).astype(f32)[:, None]
    upstream = upstream.astype(f32) * live
    grad_sum_two, grad_gain_two, grad_shift_two = norm_backward(
        upstream, scaled_two, inverse_two, vectors[4]
    )
    grad_shrunk_own = grad_sum_two.astype(bf16)
    grad_shrunk = gather_tokens(grad_shrunk_own)
    grad_shrunk, out = lax.optimization_barrier((grad_shrunk, final.astype(bf16)))
    grad_pre, sum_hidden, keep, send = hidden_backward(grad_shrunk, hidden_all, slope)
    out = to_own_features(out)
    cut = heads * HEAD // 2
    steps = heads // 4
    spare = sum_hidden.reshape(4, cols, units)
    v = Held(
        grad_pre=grad_pre, hidden=hidden, normed=normed_low, g=grad_shrunk, inputs=inputs,
        attended=attended, queries=queries, keys_values=keys_values, lse=lse,
        far_keys_values=far_keys_values, keep=keep, send=send, sum_two=grad_sum_two,
        scaled_one=scaled_one, inverse_one=inverse_one, out=out, shrunk_own=grad_shrunk_own,
        sum_two_rows=(grad_gain_two, grad_shift_two), spare=spare, vectors=vectors,
        weight_merge=weight_merge, weight_queries=weight_queries,
        weight_keys_values=weight_keys_values,
    )

    v = step_of(v)
    v.got = pair(v.send, "row")
    hidden_grads = hidden_weights(
        v.grad_pre, v.hidden, v.normed, v.g, v.spare, hidden_all.shape
    )
    hidden_sums = lax.psum_scatter(
        hidden_grads.reshape(-1, D), ("outer", "core", "col"), scatter_dimension=0, tiled=True
    )
    v = step_of(v)
    grad_normed = v.sum_two + (v.keep + v.got.astype(f32))
    res, grad_gain_one, grad_shift_one = norm_backward(
        grad_normed, v.scaled_one, v.inverse_one, v.vectors[1]
    )
    branch_own = res.astype(bf16)
    branch_got = pair(branch_own, "row")
    sum_rows = jnp.stack(
        (
            jnp.sum(branch_own, axis=0, dtype=f32),
            grad_gain_one,
            grad_shift_one,
            jnp.sum(v.shrunk_own, axis=0, dtype=f32),
            *v.sum_two_rows,
        )
    )
    v = Held(
        inputs=v.inputs, attended=v.attended, queries=v.queries, out=v.out,
        keys_values=v.keys_values, far_keys_values=v.far_keys_values, lse=v.lse,
        weight_merge=v.weight_merge, weight_queries=v.weight_queries,
        weight_keys_values=v.weight_keys_values,
    )
    v.branch = jnp.concatenate((branch_own, branch_got), 0)
    v.grad_attended = nt(v.branch, v.weight_merge, bf16)
    v.sum_rows = sum_rows
    middle = D // 2
    v.res_mine = jnp.where(row == 0, res[:, :middle], res[:, middle:])
    v.res_send = halves(jnp.where(row == 0, res[:, middle:], res[:, :middle]))
    v = step_of(v)
    shared = (
        v.queries, v.keys_values, v.far_keys_values, v.grad_attended, segment_row,
        segment_column, v.lse,
    )
    v.second = attend_backward(*shared, steps, steps)
    v.res_got = [pair(v.res_send[0], "row")]
    v = step_of(v)
    shared = (
        v.queries, v.keys_values, v.far_keys_values, v.grad_attended, segment_row,
        segment_column, v.lse,
    )
    v.far = pair(v.second[2], "core")
    v.first = attend_backward(*shared, 0, steps)
    v.res_got.append(pair(v.res_send[1], "row"))
    v = step_of(v)
    far = pair(v.first[2], "core")
    dkv_second = (v.second[1] + v.far).astype(bf16)
    v.grad_queries = jnp.concatenate((v.first[0], v.second[0]), 0)
    v.entry = tn(v.grad_queries, v.weight_queries)
    dkv_first = (v.first[1] + far).astype(bf16)
    v.grad_keys_values = jnp.concatenate((dkv_first, dkv_second), 1)
    v = step_of(v)
    which = core.reshape(1)
    part = (v.grad_keys_values, v.grad_queries, v.attended, v.inputs, v.branch)
    v.far = attend_far_weights((1 - core).reshape(1), *part, cols)
    v = step_of(v)
    v.far = pair(v.far, "core")
    entry = v.entry + nn(v.grad_keys_values, v.weight_keys_values)
    v.res_columns = by_place(row, v.res_mine, jnp.concatenate(v.res_got, 0), 0)
    v.entry_keep = jnp.where(row == 0, entry[:, :middle], entry[:, middle:])
    v.entry_send = jnp.where(row == 0, entry[:, middle:], entry[:, :middle]).astype(bf16)
    v = step_of(v)
    part = (v.grad_keys_values, v.grad_queries, v.attended, v.inputs, v.branch)
    v.mates = attend_weights(which, *part, 1, cols, bf16, v.far)
    v = step_of(v)
    part = (v.grad_keys_values, v.grad_queries, v.attended, v.inputs, v.branch)
    v.got = {2: pair(v.mates[2], "outer")}
    v.entry_got = pair(v.entry_send, "row")
    v.own = attend_weights(which, *part, 0, cols, f32, v.far)
    sum_queries = jnp.sum(v.grad_queries, axis=1, dtype=f32)
    sum_values = jnp.sum(v.grad_keys_values, axis=0, dtype=f32).reshape(heads, 2, HEAD)[:, 1]
    sum_pair = jnp.stack((sum_queries, sum_values.reshape(-1))).reshape(2, 2, cols, HEAD)
    sum_pair = flip(sum_pair.transpose(2, 0, 1, 3), 2, outer).reshape(cols, -1)
    length = sum_pair.shape[1]
    sum_pair = jnp.concatenate(
        [
            lax.dynamic_index_in_dim(sum_pair, (col - place_of) % cols, 0, keepdims=False)
            for place_of in range(cols)
        ]
    )
    v.total = jnp.concatenate((sum_pair, v.sum_rows.reshape(-1)))
    v = step_of(v)

    def to_send(sums, got, step):
        return (sums[step] + got.astype(f32)).astype(bf16)

    got = v.got
    got[1], got[3] = pair(v.mates[1], "outer"), pair(v.mates[3], "outer")
    v.two = shift(to_send(v.own, got[2], 2), -2)
    total = v.total
    v.total = total + lax.ppermute(total, "col", [(i, i ^ 1) for i in range(cols)])
    entry = jnp.roll(v.entry_got.astype(f32), own, axis=0)
    v.grad_tokens = own_first(v.entry_keep + entry) + v.res_columns
    v = step_of(v)
    v.one = to_send(v.own, v.got[1], 1)
    v.three = to_send(v.own, v.got[3], 3)
    v = step_of(v)
    v.one, v.three = shift(v.one, -1), shift(v.three, -3)
    v.got[0] = pair(v.mates[0], "outer")
    total = v.total
    v.total = total + lax.ppermute(total, "col", [(i, i ^ 2) for i in range(cols)])
    v = step_of(v)
    attend_rest = v.own[0] + v.got[0].astype(f32)
    for term in (v.one, v.two, v.three):
        attend_rest = attend_rest + term.astype(f32)
    v = step_of(
        Held(
            rest=attend_rest, hidden=hidden_sums, total=v.total, out=v.out,
            grad_tokens=v.grad_tokens,
        )
    )
    v.out = swap_sequences(v.out)
    v.block = collect_row(v.hidden)
    v.total = v.total + pair(v.total, "core")
    v = step_of(v)
    v.block_got = pair(v.block, "outer")
    v.grad_tokens = swap_sequences(v.grad_tokens)
    v.attend = collect_row(v.rest)
    v = step_of(v)
    v.block = by_place(outer, v.block[:, None], v.block_got[:, None], 1)
    v = step_of(v)
    v.attend_got = pair(v.attend, "outer")
    v.total_got = pair(v.total, "outer")
    v.block_got = pair(v.block, "core")
    v = step_of(v)
    total = v.total + v.total_got
    layer_out, grad_tokens = v.out, v.grad_tokens
    attend = by_place(outer, v.attend[:, None], v.attend_got[:, None], 1)
    attend_got = pair(attend, "core")
    grad_expand, grad_shrink, grad_expand_bias = hidden_gradients(which, v.block, v.block_got)
    attend = by_place(core, attend[:, :, None], attend_got[:, :, None], 2).astype(f32)
    grad_triple, grad_merge = ungroup(attend)
    mine = lax.dynamic_slice_in_dim(total, col * length, length)
    sum_rows = total[cols * length :].reshape(6, 2, row_size)
    low, high = sum_rows[:, 0].reshape(-1), sum_rows[:, 1].reshape(-1)
    got = pair(jnp.concatenate((mine, jnp.where(row == 0, high, low))), "row")
    totals = (jnp.where(row == 0, low, high) + got[length:]).reshape(6, row_size)
    got = got[:length]
    short = 2 * HEAD
    grad_pair = by_place(
        row, mine[: 2 * short].reshape(2, short), got[: 2 * short].reshape(2, short), 1
    )
    return (
        layer_out, grad_tokens, grad_triple, grad_pair, grad_merge, totals[0], totals[1], totals[2],
        grad_expand, grad_expand_bias, grad_shrink, totals[3], totals[4], totals[5],
    )


def masked(scores, query_segment, key_segment):
    same = query_segment[:, None] == key_segment[None, :]
    return jnp.where(same[None], scores, masked_score)


def attention_forward(queries, keys, values, query_segment, key_segment):
    scores = jnp.einsum("qhd,khd->hqk", queries, keys, preferred_element_type=f32)
    scores = masked(scores * HEAD**-0.5, query_segment, key_segment)
    top = jnp.max(scores, axis=-1, keepdims=True)
    weights = jnp.exp(scores - top)
    total = jnp.sum(weights, axis=-1, keepdims=True)
    low = (weights / total).astype(bf16)
    attended = jnp.einsum("hqk,khd->qhd", low, values, preferred_element_type=f32)
    return attended.astype(bf16), top + jnp.log(total)


def attention_backward(queries, keys, values, query_segment, key_segment, lse, grad):
    scores = jnp.einsum("qhd,khd->hqk", queries, keys, preferred_element_type=f32)
    scores = masked(scores * HEAD**-0.5, query_segment, key_segment)
    weights = jnp.exp(scores - lse)
    grad_weights = jnp.einsum("qhd,khd->hqk", grad, values, preferred_element_type=f32)
    inner = jnp.sum(weights * grad_weights, axis=-1, keepdims=True)
    grad_scores = (weights * (grad_weights - inner)).astype(bf16)
    scale = HEAD**-0.5
    grad_queries = jnp.einsum("hqk,khd->qhd", grad_scores, keys, preferred_element_type=f32) * scale
    grad_keys = jnp.einsum("hqk,qhd->khd", grad_scores, queries, preferred_element_type=f32) * scale
    grad_values = jnp.einsum(
        "hqk,qhd->khd", weights.astype(bf16), grad, preferred_element_type=f32
    )
    return grad_queries.astype(bf16), grad_keys, grad_values


def norm_forward(values, gain, shift):
    center = jnp.mean(values, axis=1, keepdims=True)
    inverse = lax.rsqrt(
        jnp.mean(values * values, axis=1, keepdims=True) - center * center + epsilon
    )
    scaled = (values - center) * inverse
    return scaled, inverse, scaled * gain + shift


def norm_backward(upstream, scaled, inverse, gain):
    through = upstream * gain
    grad = inverse * (
        through
        - jnp.mean(through, axis=1, keepdims=True)
        - scaled * jnp.mean(through * scaled, axis=1, keepdims=True)
    )
    return grad, jnp.sum(upstream * scaled, axis=0), jnp.sum(upstream, axis=0)


def exact_gelu(values):
    return jax.nn.gelu(values, approximate=False)


def layer_anywhere(
    tokens,
    segments,
    triple_weight,
    pair_bias,
    merge_weight,
    merge_bias,
    first_gain,
    first_shift,
    expand_weight,
    expand_bias,
    shrink_weight,
    shrink_bias,
    second_gain,
    second_shift,
    cotangent,
):
    rows, cols = size("row"), size("col")
    count = tokens.shape[0]
    own = count // rows
    heads = D // HEAD // rows
    row, col = place("row"), place("col")

    query_segment = lax.dynamic_slice_in_dim(segments, col * count, count)
    key_segment = query_segment

    row_size, pair_size, hidden_size = merge_bias.shape[0], pair_bias.shape[1], expand_bias.shape[0]
    row_vectors = jnp.stack(
        (merge_bias, first_gain, first_shift, shrink_bias, second_gain, second_shift)
    )
    vectors = lax.all_gather(row_vectors, "row", axis=1, tiled=True)

    def mine_of(full, axis=0):
        share = full.shape[axis] // rows
        return lax.dynamic_slice_in_dim(full, row * share, share, axis)

    bias_pair = mine_of(lax.all_gather(pair_bias, "col", axis=1, tiled=True), 1)
    bias_queries, bias_values = bias_pair[0], bias_pair[1]
    bias_hidden = mine_of(lax.all_gather(expand_bias, "col", axis=0, tiled=True)).astype(f32)
    vectors = vectors.astype(f32)

    triple = lax.all_gather(triple_weight, "col", axis=2, tiled=True)
    triple = lax.all_gather(triple, "row", axis=0, tiled=True).transpose(1, 2, 0)
    merge = lax.all_gather(merge_weight, "col", axis=0, tiled=True)
    merge = lax.all_gather(merge, "row", axis=1, tiled=True)
    expand = lax.all_gather(expand_weight, "col", axis=1, tiled=True)
    expand = lax.all_gather(expand, "row", axis=0, tiled=True).T
    shrink = lax.all_gather(shrink_weight, "col", axis=0, tiled=True)
    shrink = lax.all_gather(shrink, "row", axis=1, tiled=True)

    weight_queries, weight_keys, weight_values = (mine_of(triple[j]) for j in range(3))
    weight_merge, weight_expand, weight_shrink = mine_of(merge), mine_of(expand), mine_of(shrink)

    inputs = gather_features(tokens)
    head_shape = (-1, heads, HEAD)
    queries = (nt(inputs, weight_queries) + bias_queries.astype(f32)).astype(bf16)
    keys = nt(inputs, weight_keys).astype(bf16)
    values = (nt(inputs, weight_values) + bias_values.astype(f32)).astype(bf16)
    all_keys, all_values = keys, values
    queries_heads = queries.reshape(head_shape)
    keys_heads, values_heads = all_keys.reshape(head_shape), all_values.reshape(head_shape)
    attended, lse = attention_forward(
        queries_heads, keys_heads, values_heads, query_segment, key_segment
    )
    attended = attended.reshape(count, -1)
    branch = sum_tokens(nn(attended, weight_merge))
    residual = own_part(inputs).astype(f32) + (branch + vectors[0])
    scaled_one, inverse_one, normed_one = norm_forward(residual, vectors[1], vectors[2])
    normed_low = gather_tokens(normed_one.astype(bf16))
    pre_gelu = nt(normed_low, weight_expand) + bias_hidden
    hidden = exact_gelu(pre_gelu).astype(bf16)
    shrunk = sum_tokens(nn(hidden, weight_shrink))
    scaled_two, inverse_two, final = norm_forward(
        normed_one + (shrunk + vectors[3]), vectors[4], vectors[5]
    )

    live = (own_part(query_segment) != 0).astype(f32)[:, None]
    upstream = to_own_tokens(cotangent).astype(f32) * live
    grad_sum_two, grad_gain_two, grad_shift_two = norm_backward(
        upstream, scaled_two, inverse_two, vectors[4]
    )
    grad_shrunk_own = grad_sum_two.astype(bf16)
    grad_shrunk = gather_tokens(grad_shrunk_own)
    grad_hidden = nt(grad_shrunk, weight_shrink)
    grad_pre = jax.vjp(exact_gelu, pre_gelu)[1](grad_hidden)[0].astype(bf16)
    grad_normed = grad_sum_two + sum_tokens(nn(grad_pre, weight_expand))
    grad_res, grad_gain_one, grad_shift_one = norm_backward(
        grad_normed, scaled_one, inverse_one, vectors[1]
    )
    grad_branch_own = grad_res.astype(bf16)
    grad_branch = gather_tokens(grad_branch_own)
    grad_attended = nt(grad_branch, weight_merge).astype(bf16)
    late_out, late_res, grad_attended = lax.optimization_barrier(
        (final.astype(bf16), grad_res, grad_attended)
    )
    layer_out, grad_res_columns = to_own_features(late_out), to_own_features(late_res)
    grad_queries, grad_keys, grad_values = attention_backward(
        queries_heads,
        keys_heads,
        values_heads,
        query_segment,
        key_segment,
        lse,
        grad_attended.reshape(head_shape),
    )
    grad_queries = grad_queries.reshape(count, -1)
    grad_keys_values = jnp.concatenate(
        (grad_keys.reshape(-1, heads * HEAD), grad_values.reshape(-1, heads * HEAD)), 1
    )
    grad_keys_values = grad_keys_values.astype(bf16)
    grad_keys, grad_values = (
        grad_keys_values[:, : heads * HEAD],
        grad_keys_values[:, heads * HEAD :],
    )
    grad_entry = (
        nn(grad_queries, weight_queries)
        + nn(grad_keys, weight_keys)
        + nn(grad_values, weight_values)
    )
    grad_tokens = sum_features(grad_entry, grad_res_columns)

    def assemble(local, row_axis, col_axis):
        full = jnp.zeros((local.shape[0], local.shape[1] * rows, D), bf16)
        full = lax.dynamic_update_slice(
            full, local.astype(bf16), (0, row * local.shape[1], 0)
        )
        full = lax.psum_scatter(full, "row", scatter_dimension=2, tiled=True)
        full = lax.psum_scatter(full, "col", scatter_dimension=1, tiled=True)
        return lax.psum(full, ("outer", "core")).astype(f32)

    grad_triple = assemble(
        jnp.stack(
            (tn(grad_queries, inputs), tn(grad_keys, inputs), tn(grad_values, inputs))
        ),
        0,
        2,
    ).transpose(2, 0, 1)
    grad_merge = assemble(tn(attended, grad_branch)[None], 1, 0)[0]
    grad_expand = assemble(tn(grad_pre, normed_low)[None], 0, 1)[0].T
    grad_shrink = assemble(tn(hidden, grad_shrunk)[None], 1, 0)[0]

    def column_sums(values):
        return jnp.sum(values, axis=0, dtype=f32)

    sum_hidden = column_sums(grad_pre)
    sum_queries, sum_values = column_sums(grad_queries), column_sums(grad_values)
    sum_rows = jnp.stack(
        (
            column_sums(grad_branch_own),
            grad_gain_one,
            grad_shift_one,
            column_sums(grad_shrunk_own),
            grad_gain_two,
            grad_shift_two,
        )
    )
    everywhere = ("outer", "core", "col")
    row_totals = lax.psum_scatter(sum_rows, "row", scatter_dimension=1, tiled=True)
    row_totals = lax.psum(row_totals, everywhere)

    def whole(local):
        full = jnp.zeros(local.shape[:-1] + (local.shape[-1] * rows,), f32)
        full = lax.dynamic_update_slice_in_dim(full, local, row * local.shape[-1], -1)
        full = lax.psum(full, everywhere + ("row",))
        share = full.shape[-1] // cols
        return lax.dynamic_slice_in_dim(full, col * share, share, -1)

    grad_pair = whole(jnp.stack((sum_queries, sum_values)))
    grad_expand_bias = whole(sum_hidden)

    return (
        layer_out,
        grad_tokens,
        grad_triple,
        grad_pair,
        grad_merge,
        row_totals[0],
        row_totals[1],
        row_totals[2],
        grad_expand,
        grad_expand_bias,
        grad_shrink,
        row_totals[3],
        row_totals[4],
        row_totals[5],
    )


def shards(tokens, *others):
    sizes = [size(axis) for axis in ("outer", "core", "row", "col")]
    if sizes == [2, 2, 2, 4] and 2 * tokens.shape[0] == LEN:
        return layer(tokens, *others)
    return layer_anywhere(tokens, *others)


def solution(mesh):
    sizes = mesh.shape
    axes = ("outer", "core", "row", "col")
    split = Mesh(
        mesh.devices.reshape(sizes["dp"] // 2, 2, sizes["row"], sizes["col"]), axes
    )
    dp = ("outer", "core")
    activations = P(("outer", "core", "col"), "row")
    return jax.shard_map(
        shards,
        mesh=split,
        in_specs=(
            activations,
            P(dp),
            P("row", None, "col"),
            P(None, "col"),
            P("col", "row"),
            P("row"),
            P("row"),
            P("row"),
            P("row", "col"),
            P("col"),
            P("col", "row"),
            P("row"),
            P("row"),
            P("row"),
            activations,
        ),
        out_specs=(
            activations,
            activations,
            P("row", None, "col"),
            P(None, "col"),
            P("col", "row"),
            P("row"),
            P("row"),
            P("row"),
            P("row", "col"),
            P("col"),
            P("col", "row"),
            P("row"),
            P("row"),
            P("row"),
        ),
        check_vma=False,
    )
```

profile of v0, /device:TPU:0, one launch (start us, length us, event | category | flops | bytes accessed | tf_op | source)
XLA Modules:
  0.0 384.3 jit_solution(8357216027032071372)
XLA Ops:
  18.3 5.4 %collective-permute-done = bf16[256,512]{1,0:T(8,128)(2,1)S(1)} collective-permute-done((bf16[256,512]{1,0:T(8,128)(2,1)S(1)}, bf16[256,512]{1,0:T(8,128)(2,1)S(1)}, u32[]{:S(2)}, u32[]{:S(2)}) %collective-permute-start) | collective-permute-done | bytes 262176 | tf_op jit(solution)/shard_map/ppermute | solution.py:28
  26.4 5.3 %collective-permute-start.5 = (bf16[136,1024]{1,0:T(8,128)(2,1)S(1)}, bf16[136,1024]{1,0:T(8,128)(2,1)S(1)}, u32[]{:S(2)}, u32[]{:S(2)}) collective-permute-start(bf16[136,1024]{1,0:T(8,128)(2,1)S(1)} %fusion.11), channel_id=1, source_target_pairs={{0,1},{1,2},{2,3},{3,0},{4,5},{5,6},{6,7},{7,4},{8,9},{9,10},{10,1... | collective-permute-start | bytes 835592 | tf_op jit(solution)/shard_map/ppermute | solution.py:41
  33.8 7.5 %collective-permute-done.5 = bf16[136,1024]{1,0:T(8,128)(2,1)S(1)} collective-permute-done((bf16[136,1024]{1,0:T(8,128)(2,1)S(1)}, bf16[136,1024]{1,0:T(8,128)(2,1)S(1)}, u32[]{:S(2)}, u32[]{:S(2)}) %collective-permute-start.5) | collective-permute-done | bytes 278560 | tf_op jit(solution)/shard_map/ppermute | solution.py:41
  41.4 4.2 %collective-permute-done.6 = bf16[136,1024]{1,0:T(8,128)(2,1)S(1)} collective-permute-done((bf16[136,1024]{1,0:T(8,128)(2,1)S(1)}, bf16[136,1024]{1,0:T(8,128)(2,1)S(1)}, u32[]{:S(2)}, u32[]{:S(2)}) %collective-permute-start.6) | collective-permute-done | bytes 278560 | tf_op jit(solution)/shard_map/ppermute | solution.py:41
  50.4 3.3 collective-permute-done.11
  53.7 20.9 %collective-permute-done.10 = bf16[136,1024]{1,0:T(8,128)(2,1)S(1)} collective-permute-done((bf16[136,1024]{1,0:T(8,128)(2,1)S(1)}, bf16[136,1024]{1,0:T(8,128)(2,1)S(1)}, u32[]{:S(2)}, u32[]{:S(2)}) %collective-permute-start.10) | collective-permute-done | bytes 278560 | tf_op jit(solution)/shard_map/ppermute | solution.py:41
  76.2 5.1 %collective-permute-done.12 = bf16[136,1024]{1,0:T(8,128)(2,1)S(1)} collective-permute-done((bf16[136,1024]{1,0:T(8,128)(2,1)S(1)}, bf16[136,1024]{1,0:T(8,128)(2,1)S(1)}, u32[]{:S(2)}, u32[]{:S(2)}) %collective-permute-start.12) | collective-permute-done | bytes 278560 | tf_op jit(solution)/shard_map/ppermute | solution.py:28
  96.9 10.1 %shard_map.254 = (bf16[512,512]{1,0:T(8,128)(2,1)S(1)}, f32[4,2,512]{2,1,0:T(2,128)S(1)}) custom-call(bf16[512,512]{1,0:T(8,128)(2,1)S(1)} %fusion.q_ref, bf16[512,1024]{1,0:T(8,128)(2,1)S(1)} %add_convert_fusion.near_ref.kv_ref, bf16[512,1024]{1,0:T(8,128)(2,1)} %collective-permute-done.15.far_ref.far_kv_ref, s32[1,512]{1,0:T(1,128)S(1)} %get-tuple-element.693.qs_ref, ...), custom_call_target="tpu_custom_call" | custom-call | flops 4294967296 | bytes 4194304 | tf_op jit(solution)/shard_map/pallas_call | solution.py:270
  108.0 14.0 %collective-permute-done.16 = bf16[256,1024]{1,0:T(8,128)(2,1)S(1)} collective-permute-done((bf16[256,1024]{1,0:T(8,128)(2,1)S(1)}, bf16[256,1024]{1,0:T(8,128)(2,1)S(1)}, u32[]{:S(2)}, u32[]{:S(2)}) %collective-permute-start.16) | collective-permute-done | bytes 524320 | tf_op jit(solution)/shard_map/ppermute | solution.py:28
  125.4 11.6 %collective-permute-done.17 = bf16[256,1024]{1,0:T(8,128)(2,1)S(1)} collective-permute-done((bf16[256,1024]{1,0:T(8,128)(2,1)S(1)}, bf16[256,1024]{1,0:T(8,128)(2,1)S(1)}, u32[]{:S(2)}, u32[]{:S(2)}) %collective-permute-start.17) | collective-permute-done | bytes 524320 | tf_op jit(solution)/shard_map/ppermute | solution.py:28
  140.2 3.4 copy-done.12
  143.7 7.7 %shard_map.255 = (bf16[512,2048]{1,0:T(8,128)(2,1)S(1)}, f32[512,2048]{1,0:T(8,128)S(1)}, f32[256,1024]{1,0:T(8,128)S(1)}, bf16[256,1024]{1,0:T(8,128)(2,1)S(1)}) custom-call(bf16[512,1024]{1,0:T(8,128)(2,1)S(1)} %pad_maximum_fusion.1.x_ref, f32[4,1,512]{2,1,0:T(1,128)S(1)} %convert.10.bias_ref, bf16[2,2,4,264,1024]{4,3,2,1,0:T(8,128)(2,1)S(1)} %bitcast.144), custom_call_target="tpu_custom_call" | custom-call | flops 4294967296 | bytes 20971520 | tf_op jit(solution)/shard_map/pallas_call | solution.py:509
  153.6 10.4 %collective-permute-done.20 = bf16[256,1024]{1,0:T(8,128)(2,1)S(1)} collective-permute-done((bf16[256,1024]{1,0:T(8,128)(2,1)S(1)}, bf16[256,1024]{1,0:T(8,128)(2,1)S(1)}, u32[]{:S(2)}, u32[]{:S(2)}) %collective-permute-start.20) | collective-permute-done | bytes 524320 | tf_op jit(solution)/shard_map/ppermute | solution.py:28
  168.2 10.2 %collective-permute-done.21 = bf16[256,1024]{1,0:T(8,128)(2,1)S(1)} collective-permute-done((bf16[256,1024]{1,0:T(8,128)(2,1)S(1)}, bf16[256,1024]{1,0:T(8,128)(2,1)S(1)}, u32[]{:S(2)}, u32[]{:S(2)}) %collective-permute-start.21) | collective-permute-done | bytes 524320 | tf_op jit(solution)/shard_map/ppermute | solution.py:28
  180.3 6.6 %shard_map.256 = (bf16[512,2048]{1,0:T(8,128)(2,1)S(1)}, f32[4,1,512]{2,1,0:T(1,128)S(1)}, f32[256,1024]{1,0:T(8,128)S(1)}, bf16[256,1024]{1,0:T(8,128)(2,1)S(1)}) custom-call(bf16[512,1024]{1,0:T(8,128)(2,1)S(1)} %pad_maximum_fusion.2.g_ref, f32[512,2048]{1,0:T(8,128)S(1)} %get-tuple-element.402.slope_ref, bf16[2,2,4,264,1024]{4,3,2,1,0:T(8,128)(2,1)S(1)} %bitcast.145), custom_call_target="tpu_custom_call" | custom-call | flops 4294967296 | bytes 20971520 | tf_op jit(solution)/shard_map/pallas_call | solution.py:536
  187.9 5.6 %shard_map.262 = bf16[2,2,4,264,1024]{4,3,2,1,0:T(8,128)(2,1)S(1)} custom-call(bf16[512,2048]{1,0:T(8,128)(2,1)S(1)} %get-tuple-element.418.grad_ref, bf16[512,2048]{1,0:T(8,128)(2,1)S(1)} %get-tuple-element.419.hidden_ref, bf16[512,1024]{1,0:T(8,128)(2,1)S(1)} %pad_maximum_fusion.1.x_ref, bf16[512,1024]{1,0:T(8,128)(2,1)S(1)} %pad_maximum_fusion.2.g_ref, ...), custom_call_target="tpu_custom_call" | custom-call | flops 4294967296 | bytes 16777216 | tf_op jit(solution)/shard_map/pallas_call | solution.py:571
  193.5 3.4 copy-done.5
  198.3 9.0 %collective-permute-done.23 = bf16[256,1024]{1,0:T(8,128)(2,1)S(1)} collective-permute-done((bf16[256,1024]{1,0:T(8,128)(2,1)S(1)}, bf16[256,1024]{1,0:T(8,128)(2,1)S(1)}, u32[]{:S(2)}, u32[]{:S(2)}) %collective-permute-start.23) | collective-permute-done | bytes 524320 | tf_op jit(solution)/shard_map/ppermute | solution.py:28
  212.8 7.8 %collective-permute-done.24 = bf16[256,1024]{1,0:T(8,128)(2,1)} collective-permute-done((bf16[256,1024]{1,0:T(8,128)(2,1)}, bf16[256,1024]{1,0:T(8,128)(2,1)}, u32[]{:S(2)}, u32[]{:S(2)}) %collective-permute-start.24) | collective-permute-done | bytes 524320 | tf_op jit(solution)/shard_map/ppermute | solution.py:28
  224.7 8.4 %shard_map.257 = (bf16[256,512]{1,0:T(8,128)(2,1)S(1)}, f32[512,512]{1,0:T(8,128)S(1)}, f32[512,512]{1,0:T(8,128)S(1)}) custom-call(bf16[512,512]{1,0:T(8,128)(2,1)S(1)} %copy-done.23, bf16[512,1024]{1,0:T(8,128)(2,1)S(1)} %copy-done.14, bf16[512,1024]{1,0:T(8,128)(2,1)} %collective-permute-done.15.far_ref.far_kv_ref, ...), custom_call_target="tpu_custom_call" | custom-call | flops 5368709120 | bytes 8388608 | tf_op jit(solution)/shard_map/pallas_call | solution.py:328
  234.7 8.0 %shard_map.258 = (bf16[256,512]{1,0:T(8,128)(2,1)S(1)}, f32[512,512]{1,0:T(8,128)S(1)}, f32[512,512]{1,0:T(8,128)S(1)}) custom-call(bf16[512,512]{1,0:T(8,128)(2,1)S(1)} %copy-done.23, bf16[512,1024]{1,0:T(8,128)(2,1)S(1)} %copy-done.14, bf16[512,1024]{1,0:T(8,128)(2,1)} %collective-permute-done.15.far_ref.far_kv_ref, ...), custom_call_target="tpu_custom_call" | custom-call | flops 5368709120 | bytes 8388608 | tf_op jit(solution)/shard_map/pallas_call | solution.py:328
  269.7 7.8 %collective-permute-done.31 = bf16[128,1024]{1,0:T(8,128)(2,1)S(1)} collective-permute-done((bf16[128,1024]{1,0:T(8,128)(2,1)}, bf16[128,1024]{1,0:T(8,128)(2,1)S(1)}, u32[]{:S(2)}, u32[]{:S(2)}) %collective-permute-start.31) | collective-permute-done | bytes 262176 | tf_op jit(solution)/shard_map/ppermute | solution.py:28
  278.0 7.8 %collective-permute-start.35 = (bf16[128,1024]{1,0:T(8,128)(2,1)S(1)}, bf16[128,1024]{1,0:T(8,128)(2,1)S(1)}, u32[]{:S(2)}, u32[]{:S(2)}) collective-permute-start(bf16[128,1024]{1,0:T(8,128)(2,1)S(1)} %add_convert_fusion.6), channel_id=1, source_target_pairs={{0,2},{1,3},{2,0},{3,1},{4,6},{5,7},{6,4},{7,5},{8,10},{9,11},{10,... | collective-permute-start | bytes 786440 | tf_op jit(solution)/shard_map/ppermute | solution.py:41
  289.5 7.6 %collective-permute-done.34 = f32[7168]{0:T(1024)S(1)} collective-permute-done((f32[7168]{0:T(1024)S(1)}, f32[7168]{0:T(1024)S(1)}, u32[]{:S(2)}, u32[]{:S(2)}) %collective-permute-start.34) | collective-permute-done | bytes 28704 | tf_op jit(solution)/shard_map/ppermute | solution.py:881
  300.0 4.8 %collective-permute-done.33 = bf16[128,1024]{1,0:T(8,128)(2,1)S(1)} collective-permute-done((bf16[128,1024]{1,0:T(8,128)(2,1)S(1)}, bf16[128,1024]{1,0:T(8,128)(2,1)S(1)}, u32[]{:S(2)}, u32[]{:S(2)}) %collective-permute-start.33) | collective-permute-done | bytes 262176 | tf_op jit(solution)/shard_map/ppermute | solution.py:28
  308.7 12.9 %collective-permute-done.39 = f32[7168]{0:T(1024)S(1)} collective-permute-done((f32[7168]{0:T(1024)S(1)}, f32[7168]{0:T(1024)S(1)}, u32[]{:S(2)}, u32[]{:S(2)}) %collective-permute-start.39) | collective-permute-done | bytes 28704 | tf_op jit(solution)/shard_map/ppermute | solution.py:891
  321.6 3.4 collective-permute-done.38
  337.9 3.3 collective-permute-done.43
  341.2 4.6 %collective-permute-done.44 = bf16[2,264,512]{2,1,0:T(8,128)(2,1)S(1)} collective-permute-done((bf16[2,264,512]{2,1,0:T(8,128)(2,1)S(1)}, bf16[2,264,512]{2,1,0:T(8,128)(2,1)S(1)}, u32[]{:S(2)}, u32[]{:S(2)}) %collective-permute-start.44) | collective-permute-done | bytes 540704 | tf_op jit(solution)/shard_map/ppermute | solution.py:28
  346.9 8.1 %collective-permute-start.47 = (bf16[2,2,264,512]{3,2,1,0:T(8,128)(2,1)S(1)}, bf16[2,2,264,512]{3,2,1,0:T(8,128)(2,1)S(1)}, u32[]{:S(2)}, u32[]{:S(2)}) collective-permute-start(bf16[2,2,264,512]{3,2,1,0:T(8,128)(2,1)S(1)} %maximum_select_fusion.own_ref), channel_id=1, source_target_pairs={{0,8},{8,0},{1,9},{9,1},{2,10},{10,2},{3,11},{11,3},{4,12},{12,4},... | collective-permute-start | bytes 3244040 | tf_op jit(solution)/shard_map/ppermute | solution.py:28
  357.1 6.9 %collective-permute-done.48 = f32[7168]{0:T(1024)S(1)} collective-permute-done((f32[7168]{0:T(1024)S(1)}, f32[7168]{0:T(1024)S(1)}, u32[]{:S(2)}, u32[]{:S(2)}) %collective-permute-start.48) | collective-permute-done | bytes 28704 | tf_op jit(solution)/shard_map/ppermute | solution.py:28
  364.8 3.7 shard_map.263
  (376 shorter events, 129.6 us)
Async XLA Ops:
  7.2 129.8 %all-gather.3.cloned.1.call-start = ((), (), s32[]{:S(2)}) async-start(), calls=%async_computation.2 | async-start | bytes 9191424 | tf_op jit(solution)/shard_map/all_gather | solution.py:681
  23.8 21.8 %collective-permute-start.3 = (bf16[512,512]{1,0:T(8,128)(2,1)S(1)}, bf16[512,512]{1,0:T(8,128)(2,1)S(1)}, u32[]{:S(2)}, u32[]{:S(2)}) collective-permute-start(bf16[512,512]{1,0:T(8,128)(2,1)S(1)} %collective-permute-done.1), channel_id=1, source_target_pairs={{0,4},{4,0},{1,5},{5,1},{2,6},{6,2},{3,7},{7,3},{8,12},{12,8},{9,1... | collective-permute-start | bytes 1572872 | tf_op jit(solution)/shard_map/ppermute | solution.py:28
  26.4 14.9 %collective-permute-start.5 = (bf16[136,1024]{1,0:T(8,128)(2,1)S(1)}, bf16[136,1024]{1,0:T(8,128)(2,1)S(1)}, u32[]{:S(2)}, u32[]{:S(2)}) collective-permute-start(bf16[136,1024]{1,0:T(8,128)(2,1)S(1)} %fusion.11), channel_id=1, source_target_pairs={{0,1},{1,2},{2,3},{3,0},{4,5},{5,6},{6,7},{7,4},{8,9},{9,10},{10,1... | collective-permute-start | bytes 835592 | tf_op jit(solution)/shard_map/ppermute | solution.py:41
  31.8 13.8 %collective-permute-start.6 = (bf16[136,1024]{1,0:T(8,128)(2,1)S(1)}, bf16[136,1024]{1,0:T(8,128)(2,1)S(1)}, u32[]{:S(2)}, u32[]{:S(2)}) collective-permute-start(bf16[136,1024]{1,0:T(8,128)(2,1)S(1)} %fusion.11), channel_id=1, source_target_pairs={{0,3},{1,0},{2,1},{3,2},{4,7},{5,4},{6,5},{7,6},{8,11},{9,8},{10,9... | collective-permute-start | bytes 835592 | tf_op jit(solution)/shard_map/ppermute | solution.py:41
  46.5 278.7 %reduce-scatter.2.cloned.1.call-start = ((), (), s32[]{:S(2)}) async-start(), calls=%async_computation.1 | async-start | bytes 9191424 | tf_op jit(solution)/shard_map/reduce_scatter | solution.py:789
  46.7 28.0 %collective-permute-start.10 = (bf16[136,1024]{1,0:T(8,128)(2,1)S(1)}, bf16[136,1024]{1,0:T(8,128)(2,1)S(1)}, u32[]{:S(2)}, u32[]{:S(2)}) collective-permute-start(bf16[136,1024]{1,0:T(8,128)(2,1)S(1)} %fusion.11), channel_id=1, source_target_pairs={{0,2},{1,3},{2,0},{3,1},{4,6},{5,7},{6,4},{7,5},{8,10},{9,11},{10,... | collective-permute-start | bytes 835592 | tf_op jit(solution)/shard_map/ppermute | solution.py:41
  48.0 26.7 %collective-permute-start.8 = (bf16[136,1024]{1,0:T(8,128)(2,1)S(1)}, bf16[136,1024]{1,0:T(8,128)(2,1)S(1)}, u32[]{:S(2)}, u32[]{:S(2)}) collective-permute-start(bf16[136,1024]{1,0:T(8,128)(2,1)S(1)} %collective-permute-done.5), channel_id=1, source_target_pairs={{0,16},{16,0},{1,17},{17,1},{2,18},{18,2},{3,19},{19,3},{4,20},{20... | collective-permute-start | bytes 835592 | tf_op jit(solution)/shard_map/ppermute | solution.py:28
  48.6 26.1 %collective-permute-start.9 = (bf16[136,1024]{1,0:T(8,128)(2,1)S(1)}, bf16[136,1024]{1,0:T(8,128)(2,1)S(1)}, u32[]{:S(2)}, u32[]{:S(2)}) collective-permute-start(bf16[136,1024]{1,0:T(8,128)(2,1)S(1)} %collective-permute-done.6), channel_id=1, source_target_pairs={{0,16},{16,0},{1,17},{17,1},{2,18},{18,2},{3,19},{19,3},{4,20},{20... | collective-permute-start | bytes 835592 | tf_op jit(solution)/shard_map/ppermute | solution.py:28
  107.9 14.1 %collective-permute-start.16 = (bf16[256,1024]{1,0:T(8,128)(2,1)S(1)}, bf16[256,1024]{1,0:T(8,128)(2,1)S(1)}, u32[]{:S(2)}, u32[]{:S(2)}) collective-permute-start(bf16[256,1024]{1,0:T(8,128)(2,1)S(1)} %slice.516), channel_id=1, source_target_pairs={{0,4},{4,0},{1,5},{5,1},{2,6},{6,2},{3,7},{7,3},{8,12},{12,8},{9,1... | collective-permute-start | bytes 1572872 | tf_op jit(solution)/shard_map/ppermute | solution.py:28
  123.6 13.3 %collective-permute-start.17 = (bf16[256,1024]{1,0:T(8,128)(2,1)S(1)}, bf16[256,1024]{1,0:T(8,128)(2,1)S(1)}, u32[]{:S(2)}, u32[]{:S(2)}) collective-permute-start(bf16[256,1024]{1,0:T(8,128)(2,1)S(1)} %get-tuple-element.689), channel_id=1, source_target_pairs={{0,4},{4,0},{1,5},{5,1},{2,6},{6,2},{3,7},{7,3},{8,12},{12,8},{9,1... | collective-permute-start | bytes 1572872 | tf_op jit(solution)/shard_map/ppermute | solution.py:28
  123.9 13.1 %collective-permute-start.18 = (bf16[512,512]{1,0:T(8,128)(2,1)S(1)}, bf16[512,512]{1,0:T(8,128)(2,1)}, u32[]{:S(2)}, u32[]{:S(2)}) collective-permute-start(bf16[512,512]{1,0:T(8,128)(2,1)S(1)} %copy-done.58), channel_id=1, source_target_pairs={{0,0},{1,8},{2,2},{3,10},{8,1},{9,9},{10,3},{11,11},{4,4},{5,12},{... | collective-permute-start | bytes 1572872 | tf_op jit(solution)/shard_map/ppermute | solution.py:82
  139.4 12.0 %collective-permute-start.19 = (bf16[256,512]{1,0:T(8,128)(2,1)S(1)}, bf16[256,512]{1,0:T(8,128)(2,1)S(1)}, u32[]{:S(2)}, u32[]{:S(2)}) collective-permute-start(bf16[256,512]{1,0:T(8,128)(2,1)S(1)} %get-tuple-element.722), channel_id=1, source_target_pairs={{0,4},{4,0},{1,5},{5,1},{2,6},{6,2},{3,7},{7,3},{8,12},{12,8},{9,1... | collective-permute-start | bytes 786440 | tf_op jit(solution)/shard_map/ppermute | solution.py:28
  151.6 12.5 %collective-permute-start.20 = (bf16[256,1024]{1,0:T(8,128)(2,1)S(1)}, bf16[256,1024]{1,0:T(8,128)(2,1)S(1)}, u32[]{:S(2)}, u32[]{:S(2)}) collective-permute-start(bf16[256,1024]{1,0:T(8,128)(2,1)S(1)} %get-tuple-element.399), channel_id=1, source_target_pairs={{0,4},{4,0},{1,5},{5,1},{2,6},{6,2},{3,7},{7,3},{8,12},{12,8},{9,1... | collective-permute-start | bytes 1572872 | tf_op jit(solution)/shard_map/ppermute | solution.py:28
  166.5 11.9 %collective-permute-start.21 = (bf16[256,1024]{1,0:T(8,128)(2,1)S(1)}, bf16[256,1024]{1,0:T(8,128)(2,1)S(1)}, u32[]{:S(2)}, u32[]{:S(2)}) collective-permute-start(bf16[256,1024]{1,0:T(8,128)(2,1)S(1)} %get-tuple-element.452), channel_id=1, source_target_pairs={{0,4},{4,0},{1,5},{5,1},{2,6},{6,2},{3,7},{7,3},{8,12},{12,8},{9,1... | collective-permute-start | bytes 1572872 | tf_op jit(solution)/shard_map/ppermute | solution.py:28
  198.0 9.3 %collective-permute-start.23 = (bf16[256,1024]{1,0:T(8,128)(2,1)S(1)}, bf16[256,1024]{1,0:T(8,128)(2,1)S(1)}, u32[]{:S(2)}, u32[]{:S(2)}) collective-permute-start(bf16[256,1024]{1,0:T(8,128)(2,1)S(1)} %copy-done.16), channel_id=1, source_target_pairs={{0,4},{4,0},{1,5},{5,1},{2,6},{6,2},{3,7},{7,3},{8,12},{12,8},{9,1... | collective-permute-start | bytes 1572872 | tf_op jit(solution)/shard_map/ppermute | solution.py:28
  210.8 9.8 %collective-permute-start.24 = (bf16[256,1024]{1,0:T(8,128)(2,1)}, bf16[256,1024]{1,0:T(8,128)(2,1)}, u32[]{:S(2)}, u32[]{:S(2)}) collective-permute-start(bf16[256,1024]{1,0:T(8,128)(2,1)} %get-tuple-element.683), channel_id=1, source_target_pairs={{0,4},{4,0},{1,5},{5,1},{2,6},{6,2},{3,7},{7,3},{8,12},{12,8},{9,1... | collective-permute-start | bytes 1572872 | tf_op jit(solution)/shard_map/ppermute | solution.py:28
  224.0 9.1 %collective-permute-start.25 = (f32[128,512]{1,0:T(8,128)S(1)}, f32[128,512]{1,0:T(8,128)S(1)}, u32[]{:S(2)}, u32[]{:S(2)}) collective-permute-start(f32[128,512]{1,0:T(8,128)S(1)} %get-tuple-element.466), channel_id=1, source_target_pairs={{0,4},{4,0},{1,5},{5,1},{2,6},{6,2},{3,7},{7,3},{8,12},{12,8},{9,1... | collective-permute-start | bytes 786440 | tf_op jit(solution)/shard_map/ppermute | solution.py:28
  233.1 9.6 %collective-permute-start.26 = (f32[512,512]{1,0:T(8,128)S(1)}, f32[512,512]{1,0:T(8,128)S(1)}, u32[]{:S(2)}, u32[]{:S(2)}) collective-permute-start(f32[512,512]{1,0:T(8,128)S(1)} %get-tuple-element.477), channel_id=1, source_target_pairs={{0,8},{8,0},{1,9},{9,1},{2,10},{10,2},{3,11},{11,3},{4,12},{12,4},... | collective-permute-start | bytes 3145736 | tf_op jit(solution)/shard_map/ppermute | solution.py:28
  233.2 9.5 %collective-permute-start.27 = (f32[128,512]{1,0:T(8,128)S(1)}, f32[128,512]{1,0:T(8,128)S(1)}, u32[]{:S(2)}, u32[]{:S(2)}) collective-permute-start(f32[128,512]{1,0:T(8,128)S(1)} %get-tuple-element.489), channel_id=1, source_target_pairs={{0,4},{4,0},{1,5},{5,1},{2,6},{6,2},{3,7},{7,3},{8,12},{12,8},{9,1... | collective-permute-start | bytes 786440 | tf_op jit(solution)/shard_map/ppermute | solution.py:28
  263.3 14.5 %collective-permute-start.30 = (bf16[512,512]{1,0:T(8,128)(2,1)}, bf16[512,512]{1,0:T(8,128)(2,1)S(1)}, u32[]{:S(2)}, u32[]{:S(2)}) collective-permute-start(bf16[512,512]{1,0:T(8,128)(2,1)} %select_convert_fusion), channel_id=1, source_target_pairs={{0,4},{4,0},{1,5},{5,1},{2,6},{6,2},{3,7},{7,3},{8,12},{12,8},{9,1... | collective-permute-start | bytes 1572872 | tf_op jit(solution)/shard_map/ppermute | solution.py:28
  264.0 13.5 %collective-permute-start.31 = (bf16[128,1024]{1,0:T(8,128)(2,1)}, bf16[128,1024]{1,0:T(8,128)(2,1)S(1)}, u32[]{:S(2)}, u32[]{:S(2)}) collective-permute-start(bf16[128,1024]{1,0:T(8,128)(2,1)} %copy-done.21), channel_id=1, source_target_pairs={{0,16},{16,0},{1,17},{17,1},{2,18},{18,2},{3,19},{19,3},{4,20},{20... | collective-permute-start | bytes 786440 | tf_op jit(solution)/shard_map/ppermute | solution.py:28
  278.0 20.1 %collective-permute-start.35 = (bf16[128,1024]{1,0:T(8,128)(2,1)S(1)}, bf16[128,1024]{1,0:T(8,128)(2,1)S(1)}, u32[]{:S(2)}, u32[]{:S(2)}) collective-permute-start(bf16[128,1024]{1,0:T(8,128)(2,1)S(1)} %add_convert_fusion.6), channel_id=1, source_target_pairs={{0,2},{1,3},{2,0},{3,1},{4,6},{5,7},{6,4},{7,5},{8,10},{9,11},{10,... | collective-permute-start | bytes 786440 | tf_op jit(solution)/shard_map/ppermute | solution.py:41
  285.7 11.3 %collective-permute-start.34 = (f32[7168]{0:T(1024)S(1)}, f32[7168]{0:T(1024)S(1)}, u32[]{:S(2)}, u32[]{:S(2)}) collective-permute-start(f32[7168]{0:T(1024)S(1)} %constant_dynamic-update-slice_fusion.3), channel_id=1, source_target_pairs={{0,1},{1,0},{2,3},{3,2},{4,5},{5,4},{6,7},{7,6},{8,9},{9,8},{10,11... | collective-permute-start | bytes 86024 | tf_op jit(solution)/shard_map/ppermute | solution.py:881
  285.8 14.2 %collective-permute-start.32 = (bf16[128,1024]{1,0:T(8,128)(2,1)S(1)}, bf16[128,1024]{1,0:T(8,128)(2,1)S(1)}, u32[]{:S(2)}, u32[]{:S(2)}) collective-permute-start(bf16[128,1024]{1,0:T(8,128)(2,1)S(1)} %copy-done.20), channel_id=1, source_target_pairs={{0,16},{16,0},{1,17},{17,1},{2,18},{18,2},{3,19},{19,3},{4,20},{20... | collective-permute-start | bytes 786440 | tf_op jit(solution)/shard_map/ppermute | solution.py:28
  285.8 19.0 %collective-permute-start.33 = (bf16[128,1024]{1,0:T(8,128)(2,1)S(1)}, bf16[128,1024]{1,0:T(8,128)(2,1)S(1)}, u32[]{:S(2)}, u32[]{:S(2)}) collective-permute-start(bf16[128,1024]{1,0:T(8,128)(2,1)S(1)} %copy-done.18), channel_id=1, source_target_pairs={{0,16},{16,0},{1,17},{17,1},{2,18},{18,2},{3,19},{19,3},{4,20},{20... | collective-permute-start | bytes 786440 | tf_op jit(solution)/shard_map/ppermute | solution.py:28
  304.9 16.7 %collective-permute-start.36 = (bf16[128,1024]{1,0:T(8,128)(2,1)S(1)}, bf16[128,1024]{1,0:T(8,128)(2,1)S(1)}, u32[]{:S(2)}, u32[]{:S(2)}) collective-permute-start(bf16[128,1024]{1,0:T(8,128)(2,1)S(1)} %get-tuple-element.594), channel_id=1, source_target_pairs={{0,16},{16,0},{1,17},{17,1},{2,18},{18,2},{3,19},{19,3},{4,20},{20... | collective-permute-start | bytes 786440 | tf_op jit(solution)/shard_map/ppermute | solution.py:28
  305.2 16.3 %collective-permute-start.37 = (bf16[128,1024]{1,0:T(8,128)(2,1)S(1)}, bf16[128,1024]{1,0:T(8,128)(2,1)S(1)}, u32[]{:S(2)}, u32[]{:S(2)}) collective-permute-start(bf16[128,1024]{1,0:T(8,128)(2,1)S(1)} %add_convert_fusion.5), channel_id=1, source_target_pairs={{0,3},{1,0},{2,1},{3,2},{4,7},{5,4},{6,5},{7,6},{8,11},{9,8},{10,9... | collective-permute-start | bytes 786440 | tf_op jit(solution)/shard_map/ppermute | solution.py:41
  306.8 18.2 %collective-permute-start.38 = (bf16[128,1024]{1,0:T(8,128)(2,1)S(1)}, bf16[128,1024]{1,0:T(8,128)(2,1)S(1)}, u32[]{:S(2)}, u32[]{:S(2)}) collective-permute-start(bf16[128,1024]{1,0:T(8,128)(2,1)S(1)} %add_convert_fusion.4), channel_id=1, source_target_pairs={{0,1},{1,2},{2,3},{3,0},{4,5},{5,6},{6,7},{7,4},{8,9},{9,10},{10,1... | collective-permute-start | bytes 786440 | tf_op jit(solution)/shard_map/ppermute | solution.py:41
  307.4 14.2 %collective-permute-start.39 = (f32[7168]{0:T(1024)S(1)}, f32[7168]{0:T(1024)S(1)}, u32[]{:S(2)}, u32[]{:S(2)}) collective-permute-start(f32[7168]{0:T(1024)S(1)} %add.302), channel_id=1, source_target_pairs={{0,2},{1,3},{2,0},{3,1},{4,6},{5,7},{6,4},{7,5},{8,10},{9,11},{10,... | collective-permute-start | bytes 86024 | tf_op jit(solution)/shard_map/ppermute | solution.py:891
  334.8 11.0 %collective-permute-start.45 = (f32[512,512]{1,0:T(8,128)S(1)}, f32[512,512]{1,0:T(8,128)S(1)}, u32[]{:S(2)}, u32[]{:S(2)}) collective-permute-start(f32[512,512]{1,0:T(8,128)S(1)} %fusion.4), channel_id=1, source_target_pairs={{0,0},{1,8},{2,2},{3,10},{8,1},{9,9},{10,3},{11,11},{4,4},{5,12},{... | collective-permute-start | bytes 3145736 | tf_op jit(solution)/shard_map/ppermute | solution.py:82
  335.5 10.3 %collective-permute-start.44 = (bf16[2,264,512]{2,1,0:T(8,128)(2,1)S(1)}, bf16[2,264,512]{2,1,0:T(8,128)(2,1)S(1)}, u32[]{:S(2)}, u32[]{:S(2)}) collective-permute-start(bf16[2,264,512]{2,1,0:T(8,128)(2,1)S(1)} %pad_maximum_fusion.5), channel_id=1, source_target_pairs={{0,16},{16,0},{1,17},{17,1},{2,18},{18,2},{3,19},{19,3},{4,20},{20... | collective-permute-start | bytes 1622024 | tf_op jit(solution)/shard_map/ppermute | solution.py:28
  346.9 17.0 %collective-permute-start.47 = (bf16[2,2,264,512]{3,2,1,0:T(8,128)(2,1)S(1)}, bf16[2,2,264,512]{3,2,1,0:T(8,128)(2,1)S(1)}, u32[]{:S(2)}, u32[]{:S(2)}) collective-permute-start(bf16[2,2,264,512]{3,2,1,0:T(8,128)(2,1)S(1)} %maximum_select_fusion.own_ref), channel_id=1, source_target_pairs={{0,8},{8,0},{1,9},{9,1},{2,10},{10,2},{3,11},{11,3},{4,12},{12,4},... | collective-permute-start | bytes 3244040 | tf_op jit(solution)/shard_map/ppermute | solution.py:28
  (80 other events, 515.1 us)
Sparse Core Ops, SparseCore 0:
  46.6 77.8 all-gather.2
  197.1 118.1 reduce-scatter.1
where the time goes:
time: 387 us; the launch traced here: 384 us
  waiting for transfers between devices  168 us (43%)
  starting transfers between devices  65.3 us (17%)
  Pallas kernels  56.7 us (15%)
  local copies, waits for them, and re-layouts  38 us (10%)
  other arithmetic  30.4 us (8%)
  between operations  15.8 us (4%)
  matrix products  9.86 us (3%)
    ppermute x39, waiting for transfers between devices, pair(): return lax.ppermute(values, axis, [(0, 1), (1, 0)])  111 us
    ppermute x39, starting transfers between devices, pair(): return lax.ppermute(values, axis, [(0, 1), (1, 0)])  40.5 us
    ppermute x6, waiting for transfers between devices, shift(): lax.ppermute(values, 'col', [(i, (i + step) % count) for i in range(count)])  37 us
    unnamed x128, local copies, waits for them, and re-layouts  23.9 us
    ppermute x6, starting transfers between devices, shift(): lax.ppermute(values, 'col', [(i, (i + step) % count) for i in range(count)])  18.7 us
    pallas_call x2, Pallas kernels, attend_backward(): pl.pallas_call(attend_backward_kernel, grid=(steps,), in_specs=[query_blo...  16.3 us
    ppermute x1, waiting for transfers between devices, layer(): lax.ppermute(total, 'col', [(i, i ^ 2) for i in range(cols)])  12.9 us
    pallas_call x1, Pallas kernels, attend_forward(): pl.pallas_call(attend_forward_kernel, grid=(steps,), in_specs=[pl.BlockSp...  10.1 us
  transfers between devices with their start and end apart: 53, of which 27 were waited for; matrix products, arithmetic and copies ran while one was open for 12% of the time, Pallas kernels for 13%

commit v1 on v0

--- a/solution.py
+++ b/solution.py
@@ -896,28 +896,36 @@
     v = step_of(
         Held(
             rest=attend_rest, hidden=hidden_sums, total=v.total, out=v.out,
-            grad_tokens=v.grad_tokens,
+            grad_tokens=halves(v.grad_tokens),
         )
     )
-    v.out = swap_sequences(v.out)
+    v.tokens_low = swap_sequences(v.grad_tokens[0])
     v.block = collect_row(v.hidden)
     v.total = v.total + pair(v.total, "core")
     v = step_of(v)
     v.block_got = pair(v.block, "outer")
-    v.grad_tokens = swap_sequences(v.grad_tokens)
+    v.tokens_high = swap_sequences(v.grad_tokens[1])
     v.attend = collect_row(v.rest)
+    v.total = v.total + pair(v.total, "outer")
     v = step_of(v)
     v.block = by_place(outer, v.block[:, None], v.block_got[:, None], 1)
+    v.block_got = pair(v.block, "core")
     v = step_of(v)
     v.attend_got = pair(v.attend, "outer")
-    v.total_got = pair(v.total, "outer")
-    v.block_got = pair(v.block, "core")
-    v = step_of(v)
-    total = v.total + v.total_got
+    v.out = swap_sequences(v.out)
+    grad_expand, grad_shrink, grad_expand_bias = hidden_gradients(which, v.block, v.block_got)
+    v = step_of(
+        Held(
+            expand=grad_expand, shrink=grad_shrink, bias=grad_expand_bias, attend=v.attend,
+            attend_got=v.attend_got, total=v.total, out=v.out,
+            grad_tokens=jnp.concatenate((v.tokens_low, v.tokens_high), 0),
+        )
+    )
+    total = v.total
     layer_out, grad_tokens = v.out, v.grad_tokens
+    grad_expand, grad_shrink, grad_expand_bias = v.expand, v.shrink, v.bias
     attend = by_place(outer, v.attend[:, None], v.attend_got[:, None], 1)
     attend_got = pair(attend, "core")
-    grad_expand, grad_shrink, grad_expand_bias = hidden_gradients(which, v.block, v.block_got)
     attend = by_place(core, attend[:, :, None], attend_got[:, :, None], 2).astype(f32)
     grad_triple, grad_merge = ungroup(attend)
     mine = lax.dynamic_slice_in_dim(total, col * length, length)

time: 387 us -> 383 us (0.990)
    ppermute x39, starting transfers between devices: 40.5 us -> 35.7 us  [pair(): return lax.ppermute(values, axis, [(0, 1), (1, 0)])]
    unnamed x128 -> x131, local copies, waits for them, and re-layouts: 23.9 us -> 21.5 us
  transfers between devices with their start and end apart: 53 -> 54, of which waited for: 27 -> 27; matrix products, arithmetic and copies ran while one was open for 12% -> 12% of each run, Pallas kernels for 13% -> 13%
where the time goes in v1:
time: 383 us; the launch traced here: 380 us
  waiting for transfers between devices  169 us (44%)
  starting transfers between devices  62 us (16%)
  Pallas kernels  56.6 us (15%)
  local copies, waits for them, and re-layouts  35.7 us (9%)
  other arithmetic  31.4 us (8%)
  between operations  15.8 us (4%)
  matrix products  9.84 us (3%)
    ppermute x39, waiting for transfers between devices, pair(): return lax.ppermute(values, axis, [(0, 1), (1, 0)])  111 us
    ppermute x6, waiting for transfers between devices, shift(): lax.ppermute(values, 'col', [(i, (i + step) % count) for i in range(count)])  37.1 us
    ppermute x39, starting transfers between devices, pair(): return lax.ppermute(values, axis, [(0, 1), (1, 0)])  35.7 us
    unnamed x131, local copies, waits for them, and re-layouts  21.5 us
    ppermute x6, starting transfers between devices, shift(): lax.ppermute(values, 'col', [(i, (i + step) % count) for i in range(count)])  18.6 us
    pallas_call x2, Pallas kernels, attend_backward(): pl.pallas_call(attend_backward_kernel, grid=(steps,), in_specs=[query_blo...  16.3 us
    ppermute x1, waiting for transfers between devices, layer(): lax.ppermute(total, 'col', [(i, i ^ 2) for i in range(cols)])  12.9 us
    pallas_call x1, Pallas kernels, attend_forward(): pl.pallas_call(attend_forward_kernel, grid=(steps,), in_specs=[pl.BlockSp...  10.1 us
  transfers between devices with their start and end apart: 54, of which 27 were waited for; matrix products, arithmetic and copies ran while one was open for 12% of the time, Pallas kernels for 13%

profile of v1, /device:TPU:0, one launch (start us, length us, event | category | flops | bytes accessed | tf_op | source)
XLA Modules:
  0.0 380.4 jit_solution(8709445779153521031)
XLA Ops:
  10.6 3.0 collective-permute-start.2
  18.3 5.4 %collective-permute-done = bf16[256,512]{1,0:T(8,128)(2,1)S(1)} collective-permute-done((bf16[256,512]{1,0:T(8,128)(2,1)S(1)}, bf16[256,512]{1,0:T(8,128)(2,1)S(1)}, u32[]{:S(2)}, u32[]{:S(2)}) %collective-permute-start) | collective-permute-done | bytes 262176 | tf_op jit(solution)/shard_map/ppermute | solution.py:28
  26.4 5.3 %collective-permute-start.5 = (bf16[136,1024]{1,0:T(8,128)(2,1)S(1)}, bf16[136,1024]{1,0:T(8,128)(2,1)S(1)}, u32[]{:S(2)}, u32[]{:S(2)}) collective-permute-start(bf16[136,1024]{1,0:T(8,128)(2,1)S(1)} %fusion.11), channel_id=1, source_target_pairs={{0,1},{1,2},{2,3},{3,0},{4,5},{5,6},{6,7},{7,4},{8,9},{9,10},{10,1... | collective-permute-start | bytes 835592 | tf_op jit(solution)/shard_map/ppermute | solution.py:41
  33.8 7.5 %collective-permute-done.5 = bf16[136,1024]{1,0:T(8,128)(2,1)S(1)} collective-permute-done((bf16[136,1024]{1,0:T(8,128)(2,1)S(1)}, bf16[136,1024]{1,0:T(8,128)(2,1)S(1)}, u32[]{:S(2)}, u32[]{:S(2)}) %collective-permute-start.5) | collective-permute-done | bytes 278560 | tf_op jit(solution)/shard_map/ppermute | solution.py:41
  41.4 4.2 %collective-permute-done.6 = bf16[136,1024]{1,0:T(8,128)(2,1)S(1)} collective-permute-done((bf16[136,1024]{1,0:T(8,128)(2,1)S(1)}, bf16[136,1024]{1,0:T(8,128)(2,1)S(1)}, u32[]{:S(2)}, u32[]{:S(2)}) %collective-permute-start.6) | collective-permute-done | bytes 278560 | tf_op jit(solution)/shard_map/ppermute | solution.py:41
  50.4 3.3 collective-permute-done.11
  53.7 20.9 %collective-permute-done.10 = bf16[136,1024]{1,0:T(8,128)(2,1)S(1)} collective-permute-done((bf16[136,1024]{1,0:T(8,128)(2,1)S(1)}, bf16[136,1024]{1,0:T(8,128)(2,1)S(1)}, u32[]{:S(2)}, u32[]{:S(2)}) %collective-permute-start.10) | collective-permute-done | bytes 278560 | tf_op jit(solution)/shard_map/ppermute | solution.py:41
  76.2 5.1 %collective-permute-done.12 = bf16[136,1024]{1,0:T(8,128)(2,1)S(1)} collective-permute-done((bf16[136,1024]{1,0:T(8,128)(2,1)S(1)}, bf16[136,1024]{1,0:T(8,128)(2,1)S(1)}, u32[]{:S(2)}, u32[]{:S(2)}) %collective-permute-start.12) | collective-permute-done | bytes 278560 | tf_op jit(solution)/shard_map/ppermute | solution.py:28
  88.8 3.2 broadcast_select_fusion
  96.9 10.1 %shard_map.254 = (bf16[512,512]{1,0:T(8,128)(2,1)S(1)}, f32[4,2,512]{2,1,0:T(2,128)S(1)}) custom-call(bf16[512,512]{1,0:T(8,128)(2,1)S(1)} %fusion.q_ref, bf16[512,1024]{1,0:T(8,128)(2,1)S(1)} %add_convert_fusion.near_ref.kv_ref, bf16[512,1024]{1,0:T(8,128)(2,1)} %collective-permute-done.15.far_ref.far_kv_ref, s32[1,512]{1,0:T(1,128)S(1)} %get-tuple-element.703.qs_ref, ...), custom_call_target="tpu_custom_call" | custom-call | flops 4294967296 | bytes 4194304 | tf_op jit(solution)/shard_map/pallas_call | solution.py:270
  108.0 14.0 %collective-permute-done.16 = bf16[256,1024]{1,0:T(8,128)(2,1)S(1)} collective-permute-done((bf16[256,1024]{1,0:T(8,128)(2,1)S(1)}, bf16[256,1024]{1,0:T(8,128)(2,1)S(1)}, u32[]{:S(2)}, u32[]{:S(2)}) %collective-permute-start.16) | collective-permute-done | bytes 524320 | tf_op jit(solution)/shard_map/ppermute | solution.py:28
  125.4 11.6 %collective-permute-done.17 = bf16[256,1024]{1,0:T(8,128)(2,1)S(1)} collective-permute-done((bf16[256,1024]{1,0:T(8,128)(2,1)S(1)}, bf16[256,1024]{1,0:T(8,128)(2,1)S(1)}, u32[]{:S(2)}, u32[]{:S(2)}) %collective-permute-start.17) | collective-permute-done | bytes 524320 | tf_op jit(solution)/shard_map/ppermute | solution.py:28
  140.2 3.4 copy-done.12
  143.7 7.7 %shard_map.255 = (bf16[512,2048]{1,0:T(8,128)(2,1)S(1)}, f32[512,2048]{1,0:T(8,128)S(1)}, f32[256,1024]{1,0:T(8,128)S(1)}, bf16[256,1024]{1,0:T(8,128)(2,1)S(1)}) custom-call(bf16[512,1024]{1,0:T(8,128)(2,1)S(1)} %pad_maximum_fusion.1.x_ref, f32[4,1,512]{2,1,0:T(1,128)S(1)} %convert.10.bias_ref, bf16[2,2,4,264,1024]{4,3,2,1,0:T(8,128)(2,1)S(1)} %bitcast.144), custom_call_target="tpu_custom_call" | custom-call | flops 4294967296 | bytes 20971520 | tf_op jit(solution)/shard_map/pallas_call | solution.py:509
  153.6 10.4 %collective-permute-done.20 = bf16[256,1024]{1,0:T(8,128)(2,1)S(1)} collective-permute-done((bf16[256,1024]{1,0:T(8,128)(2,1)S(1)}, bf16[256,1024]{1,0:T(8,128)(2,1)S(1)}, u32[]{:S(2)}, u32[]{:S(2)}) %collective-permute-start.20) | collective-permute-done | bytes 524320 | tf_op jit(solution)/shard_map/ppermute | solution.py:28
  168.2 10.2 %collective-permute-done.21 = bf16[256,1024]{1,0:T(8,128)(2,1)S(1)} collective-permute-done((bf16[256,1024]{1,0:T(8,128)(2,1)S(1)}, bf16[256,1024]{1,0:T(8,128)(2,1)S(1)}, u32[]{:S(2)}, u32[]{:S(2)}) %collective-permute-start.21) | collective-permute-done | bytes 524320 | tf_op jit(solution)/shard_map/ppermute | solution.py:28
  180.3 6.6 %shard_map.256 = (bf16[512,2048]{1,0:T(8,128)(2,1)S(1)}, f32[4,1,512]{2,1,0:T(1,128)S(1)}, f32[256,1024]{1,0:T(8,128)S(1)}, bf16[256,1024]{1,0:T(8,128)(2,1)S(1)}) custom-call(bf16[512,1024]{1,0:T(8,128)(2,1)S(1)} %pad_maximum_fusion.2.g_ref, f32[512,2048]{1,0:T(8,128)S(1)} %get-tuple-element.407.slope_ref, bf16[2,2,4,264,1024]{4,3,2,1,0:T(8,128)(2,1)S(1)} %bitcast.145), custom_call_target="tpu_custom_call" | custom-call | flops 4294967296 | bytes 20971520 | tf_op jit(solution)/shard_map/pallas_call | solution.py:536
  187.8 5.6 %shard_map.262 = bf16[2,2,4,264,1024]{4,3,2,1,0:T(8,128)(2,1)S(1)} custom-call(bf16[512,2048]{1,0:T(8,128)(2,1)S(1)} %get-tuple-element.423.grad_ref, bf16[512,2048]{1,0:T(8,128)(2,1)S(1)} %get-tuple-element.424.hidden_ref, bf16[512,1024]{1,0:T(8,128)(2,1)S(1)} %pad_maximum_fusion.1.x_ref, bf16[512,1024]{1,0:T(8,128)(2,1)S(1)} %pad_maximum_fusion.2.g_ref, ...), custom_call_target="tpu_custom_call" | custom-call | flops 4294967296 | bytes 16777216 | tf_op jit(solution)/shard_map/pallas_call | solution.py:571
  193.5 3.4 copy-done.5
  198.2 9.0 %collective-permute-done.23 = bf16[256,1024]{1,0:T(8,128)(2,1)S(1)} collective-permute-done((bf16[256,1024]{1,0:T(8,128)(2,1)S(1)}, bf16[256,1024]{1,0:T(8,128)(2,1)S(1)}, u32[]{:S(2)}, u32[]{:S(2)}) %collective-permute-start.23) | collective-permute-done | bytes 524320 | tf_op jit(solution)/shard_map/ppermute | solution.py:28
  212.7 7.9 %collective-permute-done.24 = bf16[256,1024]{1,0:T(8,128)(2,1)} collective-permute-done((bf16[256,1024]{1,0:T(8,128)(2,1)}, bf16[256,1024]{1,0:T(8,128)(2,1)}, u32[]{:S(2)}, u32[]{:S(2)}) %collective-permute-start.24) | collective-permute-done | bytes 524320 | tf_op jit(solution)/shard_map/ppermute | solution.py:28
  224.6 8.4 %shard_map.257 = (bf16[256,512]{1,0:T(8,128)(2,1)S(1)}, f32[512,512]{1,0:T(8,128)S(1)}, f32[512,512]{1,0:T(8,128)S(1)}) custom-call(bf16[512,512]{1,0:T(8,128)(2,1)S(1)} %copy-done.23, bf16[512,1024]{1,0:T(8,128)(2,1)S(1)} %copy-done.14, bf16[512,1024]{1,0:T(8,128)(2,1)} %collective-permute-done.15.far_ref.far_kv_ref, ...), custom_call_target="tpu_custom_call" | custom-call | flops 5368709120 | bytes 8388608 | tf_op jit(solution)/shard_map/pallas_call | solution.py:328
  234.7 8.0 %shard_map.258 = (bf16[256,512]{1,0:T(8,128)(2,1)S(1)}, f32[512,512]{1,0:T(8,128)S(1)}, f32[512,512]{1,0:T(8,128)S(1)}) custom-call(bf16[512,512]{1,0:T(8,128)(2,1)S(1)} %copy-done.23, bf16[512,1024]{1,0:T(8,128)(2,1)S(1)} %copy-done.14, bf16[512,1024]{1,0:T(8,128)(2,1)} %collective-permute-done.15.far_ref.far_kv_ref, ...), custom_call_target="tpu_custom_call" | custom-call | flops 5368709120 | bytes 8388608 | tf_op jit(solution)/shard_map/pallas_call | solution.py:328
  269.5 8.0 %collective-permute-done.31 = bf16[128,1024]{1,0:T(8,128)(2,1)S(1)} collective-permute-done((bf16[128,1024]{1,0:T(8,128)(2,1)}, bf16[128,1024]{1,0:T(8,128)(2,1)S(1)}, u32[]{:S(2)}, u32[]{:S(2)}) %collective-permute-start.31) | collective-permute-done | bytes 262176 | tf_op jit(solution)/shard_map/ppermute | solution.py:28
  277.9 7.7 %collective-permute-start.35 = (bf16[128,1024]{1,0:T(8,128)(2,1)S(1)}, bf16[128,1024]{1,0:T(8,128)(2,1)S(1)}, u32[]{:S(2)}, u32[]{:S(2)}) collective-permute-start(bf16[128,1024]{1,0:T(8,128)(2,1)S(1)} %add_convert_fusion.6), channel_id=1, source_target_pairs={{0,2},{1,3},{2,0},{3,1},{4,6},{5,7},{6,4},{7,5},{8,10},{9,11},{10,... | collective-permute-start | bytes 786440 | tf_op jit(solution)/shard_map/ppermute | solution.py:41
  289.4 7.4 %collective-permute-done.34 = f32[7168]{0:T(1024)S(1)} collective-permute-done((f32[7168]{0:T(1024)S(1)}, f32[7168]{0:T(1024)S(1)}, u32[]{:S(2)}, u32[]{:S(2)}) %collective-permute-start.34) | collective-permute-done | bytes 28704 | tf_op jit(solution)/shard_map/ppermute | solution.py:881
  299.8 4.8 %collective-permute-done.33 = bf16[128,1024]{1,0:T(8,128)(2,1)S(1)} collective-permute-done((bf16[128,1024]{1,0:T(8,128)(2,1)S(1)}, bf16[128,1024]{1,0:T(8,128)(2,1)S(1)}, u32[]{:S(2)}, u32[]{:S(2)}) %collective-permute-start.33) | collective-permute-done | bytes 262176 | tf_op jit(solution)/shard_map/ppermute | solution.py:28
  308.6 12.9 %collective-permute-done.39 = f32[7168]{0:T(1024)S(1)} collective-permute-done((f32[7168]{0:T(1024)S(1)}, f32[7168]{0:T(1024)S(1)}, u32[]{:S(2)}, u32[]{:S(2)}) %collective-permute-start.39) | collective-permute-done | bytes 28704 | tf_op jit(solution)/shard_map/ppermute | solution.py:891
  321.5 3.4 collective-permute-done.38
  339.4 9.2 %collective-permute-done.46 = f32[7168]{0:T(1024)S(1)} collective-permute-done((f32[7168]{0:T(1024)S(1)}, f32[7168]{0:T(1024)S(1)}, u32[]{:S(2)}, u32[]{:S(2)}) %collective-permute-start.46) | collective-permute-done | bytes 28704 | tf_op jit(solution)/shard_map/ppermute | solution.py:28
  356.0 3.7 shard_map.263
  361.4 3.0 collective-permute-done.48
  (383 shorter events, 130.1 us)
Async XLA Ops:
  7.2 129.8 %all-gather.3.cloned.1.call-start = ((), (), s32[]{:S(2)}) async-start(), calls=%async_computation.2 | async-start | bytes 9191424 | tf_op jit(solution)/shard_map/all_gather | solution.py:681
  23.8 21.8 %collective-permute-start.3 = (bf16[512,512]{1,0:T(8,128)(2,1)S(1)}, bf16[512,512]{1,0:T(8,128)(2,1)S(1)}, u32[]{:S(2)}, u32[]{:S(2)}) collective-permute-start(bf16[512,512]{1,0:T(8,128)(2,1)S(1)} %collective-permute-done.1), channel_id=1, source_target_pairs={{0,4},{4,0},{1,5},{5,1},{2,6},{6,2},{3,7},{7,3},{8,12},{12,8},{9,1... | collective-permute-start | bytes 1572872 | tf_op jit(solution)/shard_map/ppermute | solution.py:28
  26.4 14.9 %collective-permute-start.5 = (bf16[136,1024]{1,0:T(8,128)(2,1)S(1)}, bf16[136,1024]{1,0:T(8,128)(2,1)S(1)}, u32[]{:S(2)}, u32[]{:S(2)}) collective-permute-start(bf16[136,1024]{1,0:T(8,128)(2,1)S(1)} %fusion.11), channel_id=1, source_target_pairs={{0,1},{1,2},{2,3},{3,0},{4,5},{5,6},{6,7},{7,4},{8,9},{9,10},{10,1... | collective-permute-start | bytes 835592 | tf_op jit(solution)/shard_map/ppermute | solution.py:41
  31.8 13.8 %collective-permute-start.6 = (bf16[136,1024]{1,0:T(8,128)(2,1)S(1)}, bf16[136,1024]{1,0:T(8,128)(2,1)S(1)}, u32[]{:S(2)}, u32[]{:S(2)}) collective-permute-start(bf16[136,1024]{1,0:T(8,128)(2,1)S(1)} %fusion.11), channel_id=1, source_target_pairs={{0,3},{1,0},{2,1},{3,2},{4,7},{5,4},{6,5},{7,6},{8,11},{9,8},{10,9... | collective-permute-start | bytes 835592 | tf_op jit(solution)/shard_map/ppermute | solution.py:41
  46.5 278.7 %reduce-scatter.2.cloned.1.call-start = ((), (), s32[]{:S(2)}) async-start(), calls=%async_computation.1 | async-start | bytes 9191424 | tf_op jit(solution)/shard_map/reduce_scatter | solution.py:789
  46.7 28.0 %collective-permute-start.10 = (bf16[136,1024]{1,0:T(8,128)(2,1)S(1)}, bf16[136,1024]{1,0:T(8,128)(2,1)S(1)}, u32[]{:S(2)}, u32[]{:S(2)}) collective-permute-start(bf16[136,1024]{1,0:T(8,128)(2,1)S(1)} %fusion.11), channel_id=1, source_target_pairs={{0,2},{1,3},{2,0},{3,1},{4,6},{5,7},{6,4},{7,5},{8,10},{9,11},{10,... | collective-permute-start | bytes 835592 | tf_op jit(solution)/shard_map/ppermute | solution.py:41
  48.0 26.7 %collective-permute-start.8 = (bf16[136,1024]{1,0:T(8,128)(2,1)S(1)}, bf16[136,1024]{1,0:T(8,128)(2,1)S(1)}, u32[]{:S(2)}, u32[]{:S(2)}) collective-permute-start(bf16[136,1024]{1,0:T(8,128)(2,1)S(1)} %collective-permute-done.5), channel_id=1, source_target_pairs={{0,16},{16,0},{1,17},{17,1},{2,18},{18,2},{3,19},{19,3},{4,20},{20... | collective-permute-start | bytes 835592 | tf_op jit(solution)/shard_map/ppermute | solution.py:28
  48.6 26.1 %collective-permute-start.9 = (bf16[136,1024]{1,0:T(8,128)(2,1)S(1)}, bf16[136,1024]{1,0:T(8,128)(2,1)S(1)}, u32[]{:S(2)}, u32[]{:S(2)}) collective-permute-start(bf16[136,1024]{1,0:T(8,128)(2,1)S(1)} %collective-permute-done.6), channel_id=1, source_target_pairs={{0,16},{16,0},{1,17},{17,1},{2,18},{18,2},{3,19},{19,3},{4,20},{20... | collective-permute-start | bytes 835592 | tf_op jit(solution)/shard_map/ppermute | solution.py:28
  107.9 14.1 %collective-permute-start.16 = (bf16[256,1024]{1,0:T(8,128)(2,1)S(1)}, bf16[256,1024]{1,0:T(8,128)(2,1)S(1)}, u32[]{:S(2)}, u32[]{:S(2)}) collective-permute-start(bf16[256,1024]{1,0:T(8,128)(2,1)S(1)} %slice.523), channel_id=1, source_target_pairs={{0,4},{4,0},{1,5},{5,1},{2,6},{6,2},{3,7},{7,3},{8,12},{12,8},{9,1... | collective-permute-start | bytes 1572872 | tf_op jit(solution)/shard_map/ppermute | solution.py:28
  123.6 13.3 %collective-permute-start.17 = (bf16[256,1024]{1,0:T(8,128)(2,1)S(1)}, bf16[256,1024]{1,0:T(8,128)(2,1)S(1)}, u32[]{:S(2)}, u32[]{:S(2)}) collective-permute-start(bf16[256,1024]{1,0:T(8,128)(2,1)S(1)} %get-tuple-element.699), channel_id=1, source_target_pairs={{0,4},{4,0},{1,5},{5,1},{2,6},{6,2},{3,7},{7,3},{8,12},{12,8},{9,1... | collective-permute-start | bytes 1572872 | tf_op jit(solution)/shard_map/ppermute | solution.py:28
  123.9 13.1 %collective-permute-start.18 = (bf16[512,512]{1,0:T(8,128)(2,1)S(1)}, bf16[512,512]{1,0:T(8,128)(2,1)}, u32[]{:S(2)}, u32[]{:S(2)}) collective-permute-start(bf16[512,512]{1,0:T(8,128)(2,1)S(1)} %copy-done.60), channel_id=1, source_target_pairs={{0,0},{1,8},{2,2},{3,10},{8,1},{9,9},{10,3},{11,11},{4,4},{5,12},{... | collective-permute-start | bytes 1572872 | tf_op jit(solution)/shard_map/ppermute | solution.py:82
  139.4 12.0 %collective-permute-start.19 = (bf16[256,512]{1,0:T(8,128)(2,1)S(1)}, bf16[256,512]{1,0:T(8,128)(2,1)S(1)}, u32[]{:S(2)}, u32[]{:S(2)}) collective-permute-start(bf16[256,512]{1,0:T(8,128)(2,1)S(1)} %get-tuple-element.734), channel_id=1, source_target_pairs={{0,4},{4,0},{1,5},{5,1},{2,6},{6,2},{3,7},{7,3},{8,12},{12,8},{9,1... | collective-permute-start | bytes 786440 | tf_op jit(solution)/shard_map/ppermute | solution.py:28
  151.5 12.5 %collective-permute-start.20 = (bf16[256,1024]{1,0:T(8,128)(2,1)S(1)}, bf16[256,1024]{1,0:T(8,128)(2,1)S(1)}, u32[]{:S(2)}, u32[]{:S(2)}) collective-permute-start(bf16[256,1024]{1,0:T(8,128)(2,1)S(1)} %get-tuple-element.404), channel_id=1, source_target_pairs={{0,4},{4,0},{1,5},{5,1},{2,6},{6,2},{3,7},{7,3},{8,12},{12,8},{9,1... | collective-permute-start | bytes 1572872 | tf_op jit(solution)/shard_map/ppermute | solution.py:28
  166.4 11.9 %collective-permute-start.21 = (bf16[256,1024]{1,0:T(8,128)(2,1)S(1)}, bf16[256,1024]{1,0:T(8,128)(2,1)S(1)}, u32[]{:S(2)}, u32[]{:S(2)}) collective-permute-start(bf16[256,1024]{1,0:T(8,128)(2,1)S(1)} %get-tuple-element.457), channel_id=1, source_target_pairs={{0,4},{4,0},{1,5},{5,1},{2,6},{6,2},{3,7},{7,3},{8,12},{12,8},{9,1... | collective-permute-start | bytes 1572872 | tf_op jit(solution)/shard_map/ppermute | solution.py:28
  210.8 9.8 %collective-permute-start.24 = (bf16[256,1024]{1,0:T(8,128)(2,1)}, bf16[256,1024]{1,0:T(8,128)(2,1)}, u32[]{:S(2)}, u32[]{:S(2)}) collective-permute-start(bf16[256,1024]{1,0:T(8,128)(2,1)} %get-tuple-element.693), channel_id=1, source_target_pairs={{0,4},{4,0},{1,5},{5,1},{2,6},{6,2},{3,7},{7,3},{8,12},{12,8},{9,1... | collective-permute-start | bytes 1572872 | tf_op jit(solution)/shard_map/ppermute | solution.py:28
  233.0 9.7 %collective-permute-start.26 = (f32[512,512]{1,0:T(8,128)S(1)}, f32[512,512]{1,0:T(8,128)S(1)}, u32[]{:S(2)}, u32[]{:S(2)}) collective-permute-start(f32[512,512]{1,0:T(8,128)S(1)} %get-tuple-element.482), channel_id=1, source_target_pairs={{0,8},{8,0},{1,9},{9,1},{2,10},{10,2},{3,11},{11,3},{4,12},{12,4},... | collective-permute-start | bytes 3145736 | tf_op jit(solution)/shard_map/ppermute | solution.py:28
  233.1 9.6 %collective-permute-start.27 = (f32[128,512]{1,0:T(8,128)S(1)}, f32[128,512]{1,0:T(8,128)S(1)}, u32[]{:S(2)}, u32[]{:S(2)}) collective-permute-start(f32[128,512]{1,0:T(8,128)S(1)} %get-tuple-element.494), channel_id=1, source_target_pairs={{0,4},{4,0},{1,5},{5,1},{2,6},{6,2},{3,7},{7,3},{8,12},{12,8},{9,1... | collective-permute-start | bytes 786440 | tf_op jit(solution)/shard_map/ppermute | solution.py:28
  263.3 14.6 %collective-permute-start.30 = (bf16[512,512]{1,0:T(8,128)(2,1)}, bf16[512,512]{1,0:T(8,128)(2,1)S(1)}, u32[]{:S(2)}, u32[]{:S(2)}) collective-permute-start(bf16[512,512]{1,0:T(8,128)(2,1)} %select_convert_fusion), channel_id=1, source_target_pairs={{0,4},{4,0},{1,5},{5,1},{2,6},{6,2},{3,7},{7,3},{8,12},{12,8},{9,1... | collective-permute-start | bytes 1572872 | tf_op jit(solution)/shard_map/ppermute | solution.py:28
  263.9 13.6 %collective-permute-start.31 = (bf16[128,1024]{1,0:T(8,128)(2,1)}, bf16[128,1024]{1,0:T(8,128)(2,1)S(1)}, u32[]{:S(2)}, u32[]{:S(2)}) collective-permute-start(bf16[128,1024]{1,0:T(8,128)(2,1)} %copy-done.21), channel_id=1, source_target_pairs={{0,16},{16,0},{1,17},{17,1},{2,18},{18,2},{3,19},{19,3},{4,20},{20... | collective-permute-start | bytes 786440 | tf_op jit(solution)/shard_map/ppermute | solution.py:28
  277.9 19.9 %collective-permute-start.35 = (bf16[128,1024]{1,0:T(8,128)(2,1)S(1)}, bf16[128,1024]{1,0:T(8,128)(2,1)S(1)}, u32[]{:S(2)}, u32[]{:S(2)}) collective-permute-start(bf16[128,1024]{1,0:T(8,128)(2,1)S(1)} %add_convert_fusion.6), channel_id=1, source_target_pairs={{0,2},{1,3},{2,0},{3,1},{4,6},{5,7},{6,4},{7,5},{8,10},{9,11},{10,... | collective-permute-start | bytes 786440 | tf_op jit(solution)/shard_map/ppermute | solution.py:41
  285.6 11.2 %collective-permute-start.34 = (f32[7168]{0:T(1024)S(1)}, f32[7168]{0:T(1024)S(1)}, u32[]{:S(2)}, u32[]{:S(2)}) collective-permute-start(f32[7168]{0:T(1024)S(1)} %constant_dynamic-update-slice_fusion.3), channel_id=1, source_target_pairs={{0,1},{1,0},{2,3},{3,2},{4,5},{5,4},{6,7},{7,6},{8,9},{9,8},{10,11... | collective-permute-start | bytes 86024 | tf_op jit(solution)/shard_map/ppermute | solution.py:881
  285.6 14.2 %collective-permute-start.32 = (bf16[128,1024]{1,0:T(8,128)(2,1)S(1)}, bf16[128,1024]{1,0:T(8,128)(2,1)S(1)}, u32[]{:S(2)}, u32[]{:S(2)}) collective-permute-start(bf16[128,1024]{1,0:T(8,128)(2,1)S(1)} %copy-done.20), channel_id=1, source_target_pairs={{0,16},{16,0},{1,17},{17,1},{2,18},{18,2},{3,19},{19,3},{4,20},{20... | collective-permute-start | bytes 786440 | tf_op jit(solution)/shard_map/ppermute | solution.py:28
  285.6 19.0 %collective-permute-start.33 = (bf16[128,1024]{1,0:T(8,128)(2,1)S(1)}, bf16[128,1024]{1,0:T(8,128)(2,1)S(1)}, u32[]{:S(2)}, u32[]{:S(2)}) collective-permute-start(bf16[128,1024]{1,0:T(8,128)(2,1)S(1)} %copy-done.18), channel_id=1, source_target_pairs={{0,16},{16,0},{1,17},{17,1},{2,18},{18,2},{3,19},{19,3},{4,20},{20... | collective-permute-start | bytes 786440 | tf_op jit(solution)/shard_map/ppermute | solution.py:28
  304.8 16.7 %collective-permute-start.36 = (bf16[128,1024]{1,0:T(8,128)(2,1)S(1)}, bf16[128,1024]{1,0:T(8,128)(2,1)S(1)}, u32[]{:S(2)}, u32[]{:S(2)}) collective-permute-start(bf16[128,1024]{1,0:T(8,128)(2,1)S(1)} %get-tuple-element.599), channel_id=1, source_target_pairs={{0,16},{16,0},{1,17},{17,1},{2,18},{18,2},{3,19},{19,3},{4,20},{20... | collective-permute-start | bytes 786440 | tf_op jit(solution)/shard_map/ppermute | solution.py:28
  305.1 16.4 %collective-permute-start.37 = (bf16[128,1024]{1,0:T(8,128)(2,1)S(1)}, bf16[128,1024]{1,0:T(8,128)(2,1)S(1)}, u32[]{:S(2)}, u32[]{:S(2)}) collective-permute-start(bf16[128,1024]{1,0:T(8,128)(2,1)S(1)} %add_convert_fusion.5), channel_id=1, source_target_pairs={{0,3},{1,0},{2,1},{3,2},{4,7},{5,4},{6,5},{7,6},{8,11},{9,8},{10,9... | collective-permute-start | bytes 786440 | tf_op jit(solution)/shard_map/ppermute | solution.py:41
  306.7 18.3 %collective-permute-start.38 = (bf16[128,1024]{1,0:T(8,128)(2,1)S(1)}, bf16[128,1024]{1,0:T(8,128)(2,1)S(1)}, u32[]{:S(2)}, u32[]{:S(2)}) collective-permute-start(bf16[128,1024]{1,0:T(8,128)(2,1)S(1)} %add_convert_fusion.4), channel_id=1, source_target_pairs={{0,1},{1,2},{2,3},{3,0},{4,5},{5,6},{6,7},{7,4},{8,9},{9,10},{10,1... | collective-permute-start | bytes 786440 | tf_op jit(solution)/shard_map/ppermute | solution.py:41
  307.3 14.2 %collective-permute-start.39 = (f32[7168]{0:T(1024)S(1)}, f32[7168]{0:T(1024)S(1)}, u32[]{:S(2)}, u32[]{:S(2)}) collective-permute-start(f32[7168]{0:T(1024)S(1)} %add.302), channel_id=1, source_target_pairs={{0,2},{1,3},{2,0},{3,1},{4,6},{5,7},{6,4},{7,5},{8,10},{9,11},{10,... | collective-permute-start | bytes 86024 | tf_op jit(solution)/shard_map/ppermute | solution.py:891
  334.7 13.9 %collective-permute-start.44 = (bf16[2,264,512]{2,1,0:T(8,128)(2,1)S(1)}, bf16[2,264,512]{2,1,0:T(8,128)(2,1)S(1)}, u32[]{:S(2)}, u32[]{:S(2)}) collective-permute-start(bf16[2,264,512]{2,1,0:T(8,128)(2,1)S(1)} %pad_maximum_fusion.6), channel_id=1, source_target_pairs={{0,16},{16,0},{1,17},{17,1},{2,18},{18,2},{3,19},{19,3},{4,20},{20... | collective-permute-start | bytes 1622024 | tf_op jit(solution)/shard_map/ppermute | solution.py:28
  335.3 13.4 %collective-permute-start.45 = (f32[256,512]{1,0:T(8,128)S(1)}, f32[256,512]{1,0:T(8,128)S(1)}, u32[]{:S(2)}, u32[]{:S(2)}) collective-permute-start(f32[256,512]{1,0:T(8,128)S(1)} %get-tuple-element.623), channel_id=1, source_target_pairs={{0,0},{1,8},{2,2},{3,10},{8,1},{9,9},{10,3},{11,11},{4,4},{5,12},{... | collective-permute-start | bytes 1572872 | tf_op jit(solution)/shard_map/ppermute | solution.py:82
  336.0 12.6 %collective-permute-start.43 = (bf16[128,512]{1,0:T(8,128)(2,1)S(1)}, bf16[128,512]{1,0:T(8,128)(2,1)S(1)}, u32[]{:S(2)}, u32[]{:S(2)}) collective-permute-start(bf16[128,512]{1,0:T(8,128)(2,1)S(1)} %broadcast_select_fusion.6), channel_id=1, source_target_pairs={{0,4},{4,0},{1,5},{5,1},{2,6},{6,2},{3,7},{7,3},{8,12},{12,8},{9,1... | collective-permute-start | bytes 393224 | tf_op jit(solution)/shard_map/ppermute | solution.py:28
  337.8 10.8 %collective-permute-start.46 = (f32[7168]{0:T(1024)S(1)}, f32[7168]{0:T(1024)S(1)}, u32[]{:S(2)}, u32[]{:S(2)}) collective-permute-start(f32[7168]{0:T(1024)S(1)} %add.311), channel_id=1, source_target_pairs={{0,16},{16,0},{1,17},{17,1},{2,18},{18,2},{3,19},{19,3},{4,20},{20... | collective-permute-start | bytes 86024 | tf_op jit(solution)/shard_map/ppermute | solution.py:28
  353.8 10.6 %collective-permute-start.49 = (bf16[512,512]{1,0:T(8,128)(2,1)}, bf16[512,512]{1,0:T(8,128)(2,1)S(1)}, u32[]{:S(2)}, u32[]{:S(2)}) collective-permute-start(bf16[512,512]{1,0:T(8,128)(2,1)} %maximum_select_fusion.9), channel_id=1, source_target_pairs={{0,0},{1,8},{2,2},{3,10},{8,1},{9,9},{10,3},{11,11},{4,4},{5,12},{... | collective-permute-start | bytes 1572872 | tf_op jit(solution)/shard_map/ppermute | solution.py:82
  (83 other events, 511.4 us)
Sparse Core Ops, SparseCore 0:
  46.6 77.8 all-gather.2
  197.0 118.3 reduce-scatter.1
